TPU v7x, 256 devices: a whole 4x4x8 slice. The times are simulated.
256 devices in a mesh: patch: 4 (over x_hi, core), seq: 64 (over y, z, x_lo).
Axes of the slice: x: 4 (x_hi: 2, x_lo: 2; x = x_hi * 2 + x_lo), y: 4, z: 8, core: 2. Of those that a mesh axis runs over, the one named last changes fastest.
Arguments:
- fresh_qkv: bfloat16 [3, 4608, 192, 128], P(None, ('patch', 'seq')), as said below
- stale_kv: bfloat16 [2, 4608, 192, 128], P(None, None, 'seq'), may hold values from -6 to 6
- text_count: int32 [8], replicated, may hold values from 128 to 512
Outputs:
- attended: bfloat16 [4608, 192, 128], P(('patch', 'seq'))
- refreshed_kv: bfloat16 [2, 4608, 192, 128], P(None, None, 'seq')
Inputs may be any that keep to these rules, and one draw needn't show every extreme that they name: `fresh_qkv`: each entry lies within -100 to 100.
All inputs are finite; a program needn't handle non-finite values.
Results may differ from a plain program's by a relative error of at most 0.0049.
Values may be sent and summed in bfloat16 or wider, within the bound.
No kernel may reach another device: no remote copies, remote signals or barrier semaphores. Data moves between devices by JAX's collectives and lax.ppermute only.
A program may use at most 128 MiB of HBM per device.

v0:
```python
import math

import jax
import jax.numpy as jnp
from jax import lax
from jax.sharding import PartitionSpec as P

HEADS = 24
TXT_DEV = 2
IMG_DEV = 16


def attend(query_part, key_part, value_part, valid_counts, text_len):
    score_scale = 1.0 / math.sqrt(query_part.shape[-1])
    position = jnp.arange(key_part.shape[0])

    def per_pair(operands):
        query_rows, key_rows, value_rows, valid_text = operands
        scores = (
            lax.dot_general(
                query_rows, key_rows, (((1,), (1,)), ((), ())), preferred_element_type=jnp.float32
            )
            * score_scale
        )
        visible = (position >= text_len) | (position < valid_text)
        scores = jnp.where(visible[None, :], scores, -jnp.inf)
        highest = jnp.max(scores, axis=1, keepdims=True)
        raised = jnp.exp(scores - highest)
        weights = (raised / jnp.sum(raised, axis=1, keepdims=True)).astype(jnp.bfloat16)
        return jnp.dot(weights, value_rows, preferred_element_type=jnp.float32).astype(jnp.bfloat16)

    outputs = lax.map(
        per_pair,
        (
            jnp.moveaxis(query_part, 1, 0),
            jnp.moveaxis(key_part, 1, 0),
            jnp.moveaxis(value_part, 1, 0),
            valid_counts,
        ),
    )
    return jnp.moveaxis(outputs, 0, 1)


def per_device(fresh_qkv, stale_kv, text_count):
    seq_count = lax.axis_size("seq")
    shard_rows = fresh_qkv.shape[1]
    pairs_here = fresh_qkv.shape[2] // seq_count
    patch_len = shard_rows * seq_count
    patch_index = lax.axis_index("patch")
    first_pair = lax.axis_index("seq") * pairs_here
    exchanged = lax.all_to_all(fresh_qkv, "seq", split_axis=2, concat_axis=1, tiled=True)
    query_part = exchanged[0]
    own_kv = exchanged[1:]
    refreshed = lax.all_gather(own_kv, "patch", axis=1, tiled=True)
    merged_kv = lax.dynamic_update_slice_in_dim(stale_kv, own_kv, patch_index * patch_len, 1)
    seq_len = stale_kv.shape[1]
    text_len = TXT_DEV * seq_len // (TXT_DEV + IMG_DEV)
    image_index = (first_pair + jnp.arange(pairs_here)) // HEADS
    matches = image_index[:, None] == jnp.arange(text_count.shape[0])[None, :]
    valid_counts = jnp.sum(jnp.where(matches, text_count[None, :], 0), axis=1)
    attended_part = attend(query_part, merged_kv[0], merged_kv[1], valid_counts, text_len)
    result = lax.all_to_all(attended_part, "seq", split_axis=0, concat_axis=1, tiled=True)
    return (result, refreshed)


def solution(mesh):
    in_specs = (P(None, ("patch", "seq"), None, None), P(None, None, "seq", None), P())
    out_specs = (P(("patch", "seq"), None, None), P(None, None, "seq", None))
    return jax.shard_map(
        per_device, mesh=mesh, in_specs=in_specs, out_specs=out_specs, check_vma=False
    )
```

profile of v0, /device:TPU:4, one launch (start us, length us, event | category | flops | bytes accessed | tf_op | source)
XLA Modules:
  0.0 238.9 jit_solution(7133903145805307879)
XLA Ops:
  7.2 0.0 copy-start.1
  7.2 6.6 %copy.49 = bf16[2,4608,3,128]{3,1,2,0:T(8,128)(2,1)} copy(bf16[2,4608,3,128]{3,1,2,0:T(8,128)(2,1)} %param.6) | data formatting | bytes 14155776
  13.7 0.0 copy-done.1
  13.8 0.0 copy-start.2
  13.8 3.6 %copy.21 = bf16[3,18,192,128]{3,1,0,2:T(8,128)(2,1)} copy(bf16[3,18,192,128]{3,2,1,0:T(8,128)(2,1)S(1)} %copy-done.1) | data formatting | bytes 5308416 | tf_op args[0]
  17.3 12.7 %all-to-all-start = ((bf16[3,18,192,128]{3,1,0,2:T(8,128)(2,1)}), bf16[3,18,192,128]{3,1,0,2:T(8,128)(2,1)S(1)}, u32[]{:S(2)}, u32[]{:S(2)}) async-start(bf16[3,18,192,128]{3,1,0,2:T(8,128)(2,1)} %copy.21), calls=%async_computation | async-start | bytes 7077888 | tf_op jit(solution)/shard_map/all_to_all | solution.py:51
  30.1 0.0 all-gather.2.cloned.1.call-start
  30.1 0.0 copy-done.2
  30.2 0.2 select_reduce_fusion
  30.3 81.9 %all-to-all-done = bf16[3,18,192,128]{3,1,0,2:T(8,128)(2,1)S(1)} async-done(((bf16[3,18,192,128]{3,1,0,2:T(8,128)(2,1)}), bf16[3,18,192,128]{3,1,0,2:T(8,128)(2,1)S(1)}, u32[]{:S(2)}, u32[]{:S(2)}) %all-to-all-start) | async-done | bytes 2654240 | tf_op jit(solution)/shard_map/all_to_all | solution.py:51
  112.3 1.9 copy.36
  114.2 1.0 slice.22
  115.2 1.6 slice.21
  116.7 3.9 %copy.24 = bf16[2,64,18,3,128]{4,0,3,2,1:T(2,128)(2,1)} copy(bf16[2,64,18,3,128]{4,3,1,2,0:T(4,128)(2,1)S(1)} %slice.22) | data formatting | bytes 3538944 | tf_op jit(solution)/shard_map/slice | solution.py:53
  120.7 0.0 all-gather.2.cloned.1.call-update
  120.7 2.9 %copy_dynamic-update-slice_fusion = bf16[2,4608,3,128]{3,1,2,0:T(8,128)(2,1)} fusion(bf16[2,4608,3,128]{3,1,2,0:T(8,128)(2,1)} %copy.49, s32[]{:T(128)S(6)} %select_n.22, bf16[2,1152,3,128]{3,0,2,1:T(2,128)(2,1)} %bitcast.52), kind=kLoop, calls=%fused_computation.24 | loop fusion | bytes 3538948 | tf_op jit(solution)/shard_map/dynamic_update_slice | solution.py:55
  123.6 0.0 copy-start
  123.6 5.4 %slice_bitcast_fusion = (bf16[3,4608,128]{2,1,0:T(8,128)(2,1)}, bf16[3,4608,128]{2,1,0:T(8,128)(2,1)S(1)}) fusion(bf16[2,4608,3,128]{3,1,2,0:T(8,128)(2,1)} %copy_dynamic-update-slice_fusion), kind=kLoop, calls=%fused_computation.21 | loop fusion | bytes 14155776 | tf_op jit(solution)/shard_map/transpose | solution.py:37
  129.1 0.0 copy-done
  129.1 1.8 copy.23
  130.8 2.4 squeeze.24
  133.2 46.6 %while.12 = (s32[]{:T(128)}, bf16[3,1152,128]{2,1,0:T(8,128)(2,1)}, s32[3]{0:T(128)S(1)}, bf16[3,1152,128]{2,1,0:T(8,128)(2,1)}, bf16[3,4608,128]{2,1,0:T(8,128)...) while((s32[]{:T(128)}, bf16[3,1152,128]{2,1,0:T(8,128)(2,1)}, s32[3]{0:T(128)S(1)}, ...), condition=%wide.region_4.5_spmd.clone.clone, body=%wide.region_1.4_spmd.clone.clone.sunk | while | flops 2760535296 | bytes 66685020 | solution.py:32
  133.2 0.6 dynamic_slice.46
  133.8 0.7 fusion.24
  134.4 4.4 %fusion.25 = (f32[1152]{0:T(1024)S(1)}, f32[1152,4608]{1,0:T(8,128)S(1)}) fusion(bf16[3,4608,128]{2,1,0:T(8,128)(2,1)S(1)} %get-tuple-element.156, s32[]{:T(128)} %get-tuple-element.145, bf16[3,1152,128]{2,1,0:T(8,128)(2,1)} %get-tuple-element.155, pred[4608]{0:T(1024)(128)(4,1)S(1)} %fusion.24), kind=kOutput, calls=%fused_computation.30.clone.1 | convolution fusion | flops 1374878592 | bytes 22718976 | tf_op jit(solution)/shard_map/while/body/eval_jaxpr/dot_general | solution.py:20
  138.8 4.2 %fusion.26 = f32[1152]{0:T(1024)S(1)} fusion(f32[1152,4608]{1,0:T(8,128)S(1)} %get-tuple-element.136, f32[1152]{0:T(1024)S(1)} %get-tuple-element.137), kind=kLoop, calls=%fused_computation.5.clone.1 | loop fusion | flops 10615680 | bytes 21242880 | tf_op jit(solution)/shard_map/while/body/eval_jaxpr/reduce_sum | solution.py:29
  143.1 5.7 %fusion.27 = bf16[3,1152,128]{2,1,0:T(8,128)(2,1)} fusion(bf16[3,1152,128]{2,1,0:T(8,128)(2,1)} %get-tuple-element.146, s32[]{:T(128)} %get-tuple-element.145, f32[1152,4608]{1,0:T(8,128)S(1)} %get-tuple-element.136, f32[1152]{0:T(1024)S(1)} %fusion.26, f32[1152]{0:T(1024)S(1)} %get-tuple-element.137, bf16[3,4608,128]{2,1,0:T(8,128)(2,1)} %get-tuple-element.157), kind=kOutput, calls=%fused_computation.9.clone.1 | convolution fusion | flops 1375027200 | bytes 22718464 | tf_op jit(solution)/shard_map/while/body/eval_jaxpr/dot_general | solution.py:30
  148.8 0.6 dynamic_slice.46
  149.3 0.7 fusion.24
  150.0 4.4 %fusion.25 = (f32[1152]{0:T(1024)S(1)}, f32[1152,4608]{1,0:T(8,128)S(1)}) fusion(bf16[3,4608,128]{2,1,0:T(8,128)(2,1)S(1)} %get-tuple-element.156, s32[]{:T(128)} %get-tuple-element.145, bf16[3,1152,128]{2,1,0:T(8,128)(2,1)} %get-tuple-element.155, pred[4608]{0:T(1024)(128)(4,1)S(1)} %fusion.24), kind=kOutput, calls=%fused_computation.30.clone.1 | convolution fusion | flops 1374878592 | bytes 22718976 | tf_op jit(solution)/shard_map/while/body/eval_jaxpr/dot_general | solution.py:20
  154.4 4.2 %fusion.26 = f32[1152]{0:T(1024)S(1)} fusion(f32[1152,4608]{1,0:T(8,128)S(1)} %get-tuple-element.136, f32[1152]{0:T(1024)S(1)} %get-tuple-element.137), kind=kLoop, calls=%fused_computation.5.clone.1 | loop fusion | flops 10615680 | bytes 21242880 | tf_op jit(solution)/shard_map/while/body/eval_jaxpr/reduce_sum | solution.py:29
  158.6 5.7 %fusion.27 = bf16[3,1152,128]{2,1,0:T(8,128)(2,1)} fusion(bf16[3,1152,128]{2,1,0:T(8,128)(2,1)} %get-tuple-element.146, s32[]{:T(128)} %get-tuple-element.145, f32[1152,4608]{1,0:T(8,128)S(1)} %get-tuple-element.136, f32[1152]{0:T(1024)S(1)} %fusion.26, f32[1152]{0:T(1024)S(1)} %get-tuple-element.137, bf16[3,4608,128]{2,1,0:T(8,128)(2,1)} %get-tuple-element.157), kind=kOutput, calls=%fused_computation.9.clone.1 | convolution fusion | flops 1375027200 | bytes 22718464 | tf_op jit(solution)/shard_map/while/body/eval_jaxpr/dot_general | solution.py:30
  164.3 0.6 dynamic_slice.46
  164.9 0.7 fusion.24
  165.5 4.4 %fusion.25 = (f32[1152]{0:T(1024)S(1)}, f32[1152,4608]{1,0:T(8,128)S(1)}) fusion(bf16[3,4608,128]{2,1,0:T(8,128)(2,1)S(1)} %get-tuple-element.156, s32[]{:T(128)} %get-tuple-element.145, bf16[3,1152,128]{2,1,0:T(8,128)(2,1)} %get-tuple-element.155, pred[4608]{0:T(1024)(128)(4,1)S(1)} %fusion.24), kind=kOutput, calls=%fused_computation.30.clone.1 | convolution fusion | flops 1374878592 | bytes 22718976 | tf_op jit(solution)/shard_map/while/body/eval_jaxpr/dot_general | solution.py:20
  169.9 4.2 %fusion.26 = f32[1152]{0:T(1024)S(1)} fusion(f32[1152,4608]{1,0:T(8,128)S(1)} %get-tuple-element.136, f32[1152]{0:T(1024)S(1)} %get-tuple-element.137), kind=kLoop, calls=%fused_computation.5.clone.1 | loop fusion | flops 10615680 | bytes 21242880 | tf_op jit(solution)/shard_map/while/body/eval_jaxpr/reduce_sum | solution.py:29
  174.2 5.7 %fusion.27 = bf16[3,1152,128]{2,1,0:T(8,128)(2,1)} fusion(bf16[3,1152,128]{2,1,0:T(8,128)(2,1)} %get-tuple-element.146, s32[]{:T(128)} %get-tuple-element.145, f32[1152,4608]{1,0:T(8,128)S(1)} %get-tuple-element.136, f32[1152]{0:T(1024)S(1)} %fusion.26, f32[1152]{0:T(1024)S(1)} %get-tuple-element.137, bf16[3,4608,128]{2,1,0:T(8,128)(2,1)} %get-tuple-element.157), kind=kOutput, calls=%fused_computation.9.clone.1 | convolution fusion | flops 1375027200 | bytes 22718464 | tf_op jit(solution)/shard_map/while/body/eval_jaxpr/dot_general | solution.py:30
  179.8 5.6 %copy.38 = bf16[3,1152,128]{2,0,1:T(4,128)(2,1)S(1)} copy(bf16[3,1152,128]{2,1,0:T(8,128)(2,1)} %get-tuple-element.42) | data formatting | bytes 1769472 | tf_op jit(solution)/shard_map/while | solution.py:32
  185.4 36.9 %all_to_all.33 = bf16[1152,3,128]{2,1,0:T(4,128)(2,1)S(1)} all-to-all(bf16[1152,3,128]{2,1,0:T(4,128)(2,1)S(1)} %bitcast.59), channel_id=1, replica_groups=mesh['patch'=4,'seq'=64] {'seq'}, dimensions={0} | all-to-all | bytes 1769472 | tf_op jit(solution)/shard_map/all_to_all | solution.py:62
  222.3 0.2 copy.37
  222.5 0.8 copy.28
  223.3 1.9 all_to_all.30
  225.2 0.0 all-gather.2.cloned.1.call-done
  225.2 6.9 %copy.29 = bf16[2,4608,3,128]{3,1,2,0:T(8,128)(2,1)} copy(bf16[2,4608,3,128]{3,0,2,1:T(2,128)(2,1)} %all-gather.2.cloned.1.call-done) | data formatting | bytes 14155776
  (2 shorter events, 0.0 us)
Async XLA Ops:
  7.2 6.6 %copy-start.1 = (bf16[3,18,192,128]{3,2,1,0:T(8,128)(2,1)S(1)}, bf16[3,18,192,128]{3,2,1,0:T(8,128)(2,1)}, u32[]{:S(2)}) copy-start(bf16[3,18,192,128]{3,2,1,0:T(8,128)(2,1)} %param.5) | copy-start | bytes 7962628
  13.8 16.4 %copy-start.2 = (s32[8]{0:T(128)S(1)}, s32[8]{0:T(128)}, u32[]{:S(2)}) copy-start(s32[8]{0:T(128)} %param.7) | copy-start | bytes 100
  17.3 94.9 %all-to-all-start = ((bf16[3,18,192,128]{3,1,0,2:T(8,128)(2,1)}), bf16[3,18,192,128]{3,1,0,2:T(8,128)(2,1)S(1)}, u32[]{:S(2)}, u32[]{:S(2)}) async-start(bf16[3,18,192,128]{3,1,0,2:T(8,128)(2,1)} %copy.21), calls=%async_computation | async-start | bytes 7077888 | tf_op jit(solution)/shard_map/all_to_all | solution.py:51
  30.1 195.1 %all-gather.2.cloned.1.call-start = ((), (), s32[]{:S(2)}) async-start(), calls=%async_computation.2 | async-start | bytes 8847360 | tf_op jit(solution)/shard_map/all_gather | solution.py:54
  123.6 5.4 %copy-start = (bf16[1,64,18,3,128]{4,3,1,2,0:T(4,128)(2,1)S(1)}, bf16[1,64,18,3,128]{4,3,1,2,0:T(4,128)(2,1)}, u32[]{:S(2)}) copy-start(bf16[1,64,18,3,128]{4,3,1,2,0:T(4,128)(2,1)} %slice.21) | copy-start | bytes 2654212
Sparse Core Ops, SparseCore 0:
  120.8 50.9 all-gather.1
where the time goes:
time: 239 us
  waiting for transfers between devices  81.9 us (34%)
  local copies, waits for them, and re-layouts  48.1 us (20%)
  blocking collectives  36.9 us (15%)
  matrix products  30.2 us (13%)
  other arithmetic  14.9 us (6%)
  between operations  14.1 us (6%)
  starting transfers between devices  12.8 us (5%)
    all_to_all x1, waiting for transfers between devices, per_device(): lax.all_to_all(fresh_qkv, 'seq', split_axis=2, concat_axis=1, tiled=True)  81.9 us
    all_to_all x1, blocking collectives, per_device(): lax.all_to_all(attended_part, 'seq', split_axis=0, concat_axis=1, tiled=T...  36.9 us
    dot_general x3, matrix products, per_pair(): jnp.dot(weights, value_rows, preferred_element_type=jnp.float32)  17 us
    unnamed x9, local copies, waits for them, and re-layouts  17 us
    dot_general x3, matrix products, per_pair(): lax.dot_general(query_rows, key_rows, (((1,), (1,)), ((), ())), preferred...  13.2 us
    all_to_all x1, starting transfers between devices, per_device(): lax.all_to_all(fresh_qkv, 'seq', split_axis=2, concat_axis=1, tiled=True)  12.7 us
    reduce_sum x3, other arithmetic, per_pair(): jnp.sum(raised, axis=1, keepdims=True)  12.7 us
    while x1, local copies, waits for them, and re-layouts, attend(): lax.map(per_pair, (jnp.moveaxis(query_part, 1, 0), jnp.moveaxis(key_part,...  5.61 us
  transfers between devices with their start and end apart: 2, of which 1 were waited for; matrix products, arithmetic and copies ran while one was open for 28% of the time, Pallas kernels for 0%

commit v1 on v0

v1 whole, which is shorter than its diff:
```python
import functools
import math

import jax
import jax.numpy as jnp
from jax import lax
from jax.experimental import pallas as pl
from jax.experimental.pallas import tpu as pltpu
from jax.sharding import PartitionSpec as P

HEADS = 24
TXT_DEV = 2
IMG_DEV = 16
KINDS = 3
BLOCK = 384
MIB = 1024 * 1024
F32 = jnp.float32
VMEM = pl.BlockSpec(memory_space=pltpu.VMEM)


def cost(mib, flops=0, exps=0):
    return pl.CostEstimate(flops=flops, bytes_accessed=mib * MIB, transcendentals=exps)


def pack_kernel(here, x_ref, o_ref, read, wide, sent, packed, in_sems, out_sems):
    kinds, tokens, pairs, _ = x_ref.shape
    steps = in_sems.shape[0]
    columns = pairs // steps
    peers = columns // here
    rows = kinds * tokens * here
    reads, writes = [], []
    for i in range(steps):
        part = pl.ds(i * columns, columns)
        copy = pltpu.make_async_copy(x_ref.at[:, :, part, :], read.at[i], in_sems.at[i])
        copy.start()
        reads.append(copy)
    for i in range(steps):
        reads[i].wait()
        wide[...] = read[i].astype(F32).reshape(wide.shape)
        for c in range(kinds):
            for t in range(tokens):
                for j in range(here):
                    first = (c * tokens + t) * columns + j
                    row = (j * kinds + c) * tokens + t
                    sent[pl.ds(row, peers, stride=rows), :] = wide[pl.ds(first, peers, stride=here), :]
        packed[i] = sent[...].astype(packed.dtype)
        part = pl.ds(i * peers * rows, peers * rows)
        copy = pltpu.make_async_copy(packed.at[i], o_ref.at[part, :], out_sems.at[i])
        copy.start()
        writes.append(copy)
    for copy in writes:
        copy.wait()


PACK_STEPS = 4


def pack(fresh_qkv, peers):
    kinds, tokens, pairs, width = fresh_qkv.shape
    columns = pairs // PACK_STEPS
    part = (kinds * tokens * columns, width)
    anywhere = pl.BlockSpec(memory_space=pl.ANY)
    return pl.pallas_call(
        functools.partial(pack_kernel, pairs // peers),
        out_shape=jax.ShapeDtypeStruct((kinds * tokens * pairs, width), fresh_qkv.dtype),
        in_specs=[anywhere],
        out_specs=anywhere,
        scratch_shapes=[
            pltpu.VMEM((PACK_STEPS, kinds, tokens, columns, width), fresh_qkv.dtype),
            pltpu.VMEM(part, F32),
            pltpu.VMEM(part, F32),
            pltpu.VMEM((PACK_STEPS, *part), fresh_qkv.dtype),
            pltpu.SemaphoreType.DMA((PACK_STEPS,)),
            pltpu.SemaphoreType.DMA((PACK_STEPS,)),
        ],
        compiler_params=pltpu.CompilerParams(vmem_limit_bytes=60 * MIB),
        cost_estimate=cost(6),
        name="pack",
    )(fresh_qkv)


def unpack_kernel(kinds, x_ref, o_ref, wide, ordered):
    count, here, length, _ = o_ref.shape
    rows = KINDS * here
    total = x_ref.shape[0]
    wide[...] = x_ref[...].astype(F32)
    tokens = TOKENS
    peers = length // tokens
    for c, kind in enumerate(kinds):
        for j in range(here):
            for t in range(tokens):
                row = (j * KINDS + kind) * tokens + t
                block = wide[pl.ds(row, peers, stride=rows * tokens), :]
                ordered[c * here + j, pl.ds(t, peers, stride=tokens), :] = block
    o_ref[...] = ordered[...].reshape(o_ref.shape).astype(o_ref.dtype)


TOKENS = 18


def unpack(received, here, kinds):
    total, width = received.shape
    length = total // (KINDS * here)
    return pl.pallas_call(
        functools.partial(unpack_kernel, kinds),
        out_shape=jax.ShapeDtypeStruct((len(kinds), here, length, width), received.dtype),
        in_specs=[VMEM],
        out_specs=VMEM,
        scratch_shapes=[
            pltpu.VMEM((total, width), F32),
            pltpu.VMEM((len(kinds) * here, length, width), F32),
        ],
        compiler_params=pltpu.CompilerParams(vmem_limit_bytes=24 * MIB),
        cost_estimate=cost(5),
        name="unpack",
    )(received)


def hide_text(valid, text, keys, values, width, first):
    length = text.size
    shown = lax.broadcasted_iota(jnp.int32, (length, width), 0) < valid
    keys[text, :] = jnp.where(shown, keys[text, :].astype(F32), first).astype(keys.dtype)
    for part in range(2):
        lanes = pl.ds(part * width, width)
        values[text, lanes] = jnp.where(shown, values[text, lanes].astype(F32), 0.0).astype(values.dtype)


def prepare_kernel(text_len, scalars, stale_ref, keys, values, sems):
    pair = pl.program_id(0)
    width = keys.shape[-1]
    groups = sems.shape[1] + 1
    length = keys.shape[1] // (groups - 1)
    own = scalars[0]
    valid = scalars[1 + pair]
    copies = []
    for step in range(1, groups):
        group = lax.rem(own + step, groups)
        source = pl.ds(pl.multiple_of(group * length, length), length)
        rows = pl.ds((step - 1) * length, length)
        for which, target in ((0, keys.at[0, rows, :]), (1, values.at[0, rows, pl.ds(0, width)])):
            copy = pltpu.make_async_copy(
                stale_ref.at[which, pair, source, :], target, sems.at[which, step - 1]
            )
            copy.start()
            copies.append(copy)
    values[0, :, pl.ds(width, width)] = jnp.ones((keys.shape[1], width), values.dtype)
    for copy in copies:
        copy.wait()

    @pl.when(own > 0)
    def _():
        start = pl.multiple_of((groups - 1 - own) * length, length)
        first = keys[0, pl.ds(start, 16), :][0:1].astype(F32)
        hide_text(valid, pl.ds(start, text_len), keys.at[0], values.at[0], width, first)


def prepare(scalars, stale, groups, text_len):
    _, here, seq_len, width = stale.shape
    others = seq_len // groups * (groups - 1)
    return pl.pallas_call(
        functools.partial(prepare_kernel, text_len),
        grid=(here,),
        out_shape=[
            jax.ShapeDtypeStruct((here, others, width), stale.dtype),
            jax.ShapeDtypeStruct((here, others, 2 * width), stale.dtype),
        ],
        in_specs=[
            pl.BlockSpec(memory_space=pltpu.SMEM),
            pl.BlockSpec(memory_space=pl.ANY),
        ],
        out_specs=[
            pl.BlockSpec((1, others, width), lambda i: (i, 0, 0)),
            pl.BlockSpec((1, others, 2 * width), lambda i: (i, 0, 0)),
        ],
        scratch_shapes=[pltpu.SemaphoreType.DMA((2, groups - 1))],
        compiler_params=pltpu.CompilerParams(vmem_limit_bytes=16 * MIB),
        cost_estimate=cost(64),
        name="prepare",
    )(scalars, stale)


def attend_kernel(text_len, tokens, scalars, q_ref, fresh_ref, old_keys, old_values, o_ref,
                  keys, values, scores, highest, result, sent):
    here, length, width = q_ref.shape
    peers = length // tokens
    blocks = length // BLOCK
    scale = math.log2(math.e) / math.sqrt(width)
    own = scalars[0]
    values[:, pl.ds(width, width)] = jnp.ones((length, width), values.dtype)

    def attend_pair(pair, _):
        valid = scalars[1 + pair]
        keys[...] = fresh_ref[0, pair]
        values[:, pl.ds(0, width)] = fresh_ref[1, pair]

        @pl.when(own == 0)
        def _():
            values[pl.ds(0, text_len), pl.ds(width, width)] = jnp.ones((text_len, width), values.dtype)
            first = keys[0:16, :][0:1].astype(F32)
            hide_text(valid, pl.ds(0, text_len), keys, values, width, first)

        def score(i, slot):
            query = q_ref[pair, pl.ds(i * BLOCK, BLOCK), :]
            dims = (((1,), (1,)), ((), ()))
            new = lax.dot_general(query, keys[...], dims, preferred_element_type=F32)
            old = lax.dot_general(query, old_keys[pair], dims, preferred_element_type=F32)
            scores[slot, :, pl.ds(0, length)] = new
            scores[slot, :, pl.ds(length, old.shape[1])] = old
            top = jnp.maximum(
                jnp.max(new, axis=1, keepdims=True), jnp.max(old, axis=1, keepdims=True)
            )
            highest[slot] = jnp.broadcast_to(top, (BLOCK, width))

        def weigh(i, slot):
            top = highest[slot][:, :1]
            weights = jnp.exp2((scores[slot] - top) * scale).astype(values.dtype)
            summed = jnp.dot(weights[:, :length], values[...], preferred_element_type=F32)
            summed += jnp.dot(weights[:, length:], old_values[pair], preferred_element_type=F32)
            result[pl.ds(i * BLOCK, BLOCK), :] = summed[:, :width] / summed[:, width:]

        score(0, 0)
        for i in range(1, blocks):
            score(i, i % 2)
            weigh(i - 1, (i - 1) % 2)
        weigh(blocks - 1, (blocks - 1) % 2)
        for t in range(tokens):
            rows = pl.ds(pair * tokens + t, peers, stride=here * tokens)
            sent[rows, :] = result[pl.ds(t, peers, stride=tokens), :]
        return 0

    lax.fori_loop(0, here, attend_pair, 0)
    o_ref[...] = sent[...].astype(o_ref.dtype)


PAIRS = 3


def attend(scalars, query, fresh, old_keys, old_values, text_len, tokens):
    here, length, width = query.shape
    others = old_keys.shape[1]
    total = length + others
    return pl.pallas_call(
        functools.partial(attend_kernel, text_len, tokens),
        out_shape=jax.ShapeDtypeStruct((here * length, width), query.dtype),
        in_specs=[pl.BlockSpec(memory_space=pltpu.SMEM)] + [VMEM] * 4,
        out_specs=VMEM,
        scratch_shapes=[
            pltpu.VMEM((length, width), query.dtype),
            pltpu.VMEM((length, 2 * width), query.dtype),
            pltpu.VMEM((2, BLOCK, total), F32),
            pltpu.VMEM((2, BLOCK, width), F32),
            pltpu.VMEM((length, width), F32),
            pltpu.VMEM((here * length, width), F32),
        ],
        compiler_params=pltpu.CompilerParams(vmem_limit_bytes=40 * MIB),
        cost_estimate=cost(16, 8 * here * length * total * width, here * length * total),
        name="attend",
    )(scalars, query, fresh, old_keys, old_values)


def merge_kernel(x_ref, o_ref, wide, spread):
    tokens, pairs, _ = o_ref.shape
    here = PAIRS
    peers = pairs // here
    wide[...] = x_ref[...].astype(F32)
    for j in range(here):
        for t in range(tokens):
            block = wide[pl.ds(j * tokens + t, peers, stride=here * tokens), :]
            spread[pl.ds(t * pairs + j, peers, stride=here), :] = block
    o_ref[...] = spread[...].reshape(o_ref.shape).astype(o_ref.dtype)


def merge(moved, pairs):
    total, width = moved.shape
    return pl.pallas_call(
        merge_kernel,
        out_shape=jax.ShapeDtypeStruct((total // pairs, pairs, width), moved.dtype),
        in_specs=[VMEM],
        out_specs=VMEM,
        scratch_shapes=[pltpu.VMEM((total, width), F32)] * 2,
        compiler_params=pltpu.CompilerParams(vmem_limit_bytes=16 * MIB),
        cost_estimate=cost(2),
        name="merge",
    )(moved)


def place_kernel(scalars, *refs):
    part_refs, o_ref = refs[:-1], refs[-1]
    length = part_refs[0].shape[2]
    for step, part_ref in enumerate(part_refs):
        group = jnp.bitwise_xor(scalars[0], step)
        o_ref[0, 0, pl.ds(pl.multiple_of(group * length, length), length), :] = part_ref[0, 0]


def place(scalars, parts):
    kinds, here, length, width = parts[0].shape
    total = len(parts) * length
    block = lambda i, j: (i, j, 0, 0)
    return pl.pallas_call(
        place_kernel,
        grid=(kinds, here),
        out_shape=jax.ShapeDtypeStruct((kinds, here, total, width), parts[0].dtype),
        in_specs=[pl.BlockSpec(memory_space=pltpu.SMEM)]
        + [pl.BlockSpec((1, 1, length, width), block)] * len(parts),
        out_specs=pl.BlockSpec((1, 1, total, width), block),
        compiler_params=pltpu.CompilerParams(vmem_limit_bytes=16 * MIB),
        cost_estimate=cost(0),
        name="place",
    )(scalars, *parts)


def exchange(rows):
    two_rows = rows.reshape(rows.shape[0] // 2, 2, rows.shape[1])
    moved = lax.all_to_all(two_rows, "seq", split_axis=0, concat_axis=0, tiled=True)
    return moved.reshape(rows.shape)


def swap(array, bit):
    groups = lax.axis_size("patch")
    return lax.ppermute(array, "patch", [(g, g ^ bit) for g in range(groups)])


def per_device(fresh_qkv, stale_kv, text_count):
    peers = lax.axis_size("seq")
    groups = lax.axis_size("patch")
    tokens, pairs = fresh_qkv.shape[1:3]
    here = pairs // peers
    seq_len = stale_kv.shape[1]
    text_len = TXT_DEV * seq_len // (TXT_DEV + IMG_DEV)
    first_pair = lax.axis_index("seq") * here
    image_index = (first_pair + jnp.arange(here)) // HEADS
    matches = image_index[:, None] == jnp.arange(text_count.shape[0])[None, :]
    valid_counts = jnp.sum(jnp.where(matches, text_count[None, :], 0), axis=1)
    own = lax.axis_index("patch").astype(jnp.int32)
    scalars = jnp.concatenate([own[None], valid_counts.astype(jnp.int32)])
    stale = jnp.transpose(stale_kv, (0, 2, 1, 3))

    sent, scalars = lax.optimization_barrier((pack(fresh_qkv, peers), scalars))
    received = exchange(sent)
    old_keys, old_values = prepare(scalars, stale, groups, text_len)
    received, old_keys, old_values = lax.optimization_barrier((received, old_keys, old_values))

    fresh = unpack(received, here, (1, 2))
    far = swap(fresh, 2)
    query = unpack(received, here, (0,))[0]
    attended = attend(scalars, query, fresh, old_keys, old_values, text_len, tokens)
    moved = exchange(attended)
    far, _ = lax.optimization_barrier((far, attended))
    near, far_near = swap(fresh, 1), swap(far, 1)
    refreshed = place(scalars, [fresh, near, far, far_near])
    moved, refreshed = lax.optimization_barrier((moved, refreshed))
    result = merge(moved, pairs)
    return (result, jnp.transpose(refreshed, (0, 2, 1, 3)))


def solution(mesh):
    in_specs = (P(None, ("patch", "seq"), None, None), P(None, None, "seq", None), P())
    out_specs = (P(("patch", "seq"), None, None), P(None, None, "seq", None))
    return jax.shard_map(
        per_device, mesh=mesh, in_specs=in_specs, out_specs=out_specs, check_vma=False
    )
```

time: 239 us -> 158 us (0.66)
  local copies, waits for them, and re-layouts: 48.1 us -> 7.88 us
  Pallas kernels: 0 us -> 38.7 us
  blocking collectives: 36.9 us -> 0 us
  matrix products: 30.2 us -> 0 us
  other arithmetic: 14.9 us -> 0.27 us
  between operations: 14.1 us -> 0.75 us
  starting transfers between devices: 12.8 us -> 21.7 us
  waiting for transfers between devices: 81.9 us -> 87.8 us
    pallas_call x0 -> x7, Pallas kernels: none -> 38.7 us  [the longest x1 23 us: attend(): pl.pallas_call(functools.partial(attend_kernel, text_len, tokens), out_sh...]
    all_to_all x1 -> x0, blocking collectives: 36.9 us -> none  [per_device(): lax.all_to_all(attended_part, 'seq', split_axis=0, concat_axis=1, tiled=T...]
    dot_general x6 -> x0, matrix products: 30.2 us -> none  [the longest x3 17 us: per_pair(): jnp.dot(weights, value_rows, preferred_element_type=jnp.float32)]
    ppermute x0 -> x3, waiting for transfers between devices: none -> 14.1 us  [swap(): return lax.ppermute(array, 'patch', [(g, g ^ bit) for g in range(groups)])]
    reduce_sum x3 -> x0, other arithmetic: 12.7 us -> none  [per_pair(): jnp.sum(raised, axis=1, keepdims=True)]
    unnamed x9 -> x12, local copies, waits for them, and re-layouts: 17 us -> 7.88 us
    slice x4 -> x0, local copies, waits for them, and re-layouts: 8.27 us -> none  [the longest x2 4.93 us: per_device(): own_kv = exchanged[1:]]
    all_to_all x1 -> x2, waiting for transfers between devices: 81.9 us -> 73.7 us  [exchange(): lax.all_to_all(two_rows, 'seq', split_axis=0, concat_axis=0, tiled=True)]
  transfers between devices with their start and end apart: 2 -> 5, of which waited for: 1 -> 3; matrix products, arithmetic and copies ran while one was open for 28% -> 0% of each run, Pallas kernels for 0% -> 21%
where the time goes in v1:
time: 158 us; the launch traced here: 157 us
  waiting for transfers between devices  87.8 us (56%)
  Pallas kernels  38.7 us (24%)
  starting transfers between devices  21.7 us (14%)
  local copies, waits for them, and re-layouts  7.88 us (5%)
    all_to_all x2, waiting for transfers between devices, exchange(): lax.all_to_all(two_rows, 'seq', split_axis=0, concat_axis=0, tiled=True)  73.7 us
    pallas_call x1, Pallas kernels, attend(): pl.pallas_call(functools.partial(attend_kernel, text_len, tokens), out_sh...  23 us
    all_to_all x2, starting transfers between devices, exchange(): lax.all_to_all(two_rows, 'seq', split_axis=0, concat_axis=0, tiled=True)  20.8 us
    ppermute x3, waiting for transfers between devices, swap(): return lax.ppermute(array, 'patch', [(g, g ^ bit) for g in range(groups)])  14.1 us
    unnamed x12, local copies, waits for them, and re-layouts  7.88 us
    pallas_call x1, Pallas kernels, place(): pl.pallas_call(place_kernel, grid=(kinds, here), out_shape=jax.ShapeDtype...  6.63 us
  transfers between devices with their start and end apart: 5, of which 3 were waited for; matrix products, arithmetic and copies ran while one was open for 0% of the time, Pallas kernels for 21%

profile of v1, /device:TPU:4, one launch (start us, length us, event | category | flops | bytes accessed | tf_op | source)
XLA Modules:
  0.0 157.1 jit_solution(6743559330819377554)
XLA Ops:
  0.7 0.0 copy-start.5
  0.7 3.0 %pack.1 = bf16[10368,128]{1,0:T(8,128)(2,1)} custom-call(bf16[3,18,192,128]{3,2,1,0:T(8,128)(2,1)} %x_ref.1), custom_call_target="tpu_custom_call" | custom-call | bytes 6291456 | tf_op jit(solution)/shard_map/pack/pallas_call | solution.py:63
  3.7 0.0 copy-done.5
  3.7 0.2 select_reduce_fusion
  3.9 0.1 pad_add_fusion.scalars
  4.0 12.7 %all-to-all-start = ((bf16[5184,2,128]{2,1,0:T(2,128)(2,1)}), bf16[5184,2,128]{2,1,0:T(2,128)(2,1)S(1)}, u32[]{:S(2)}, u32[]{:S(2)}) async-start(bf16[5184,2,128]{2,1,0:T(2,128)(2,1)} %bitcast.13), calls=%async_computation | async-start | bytes 5308416 | tf_op jit(solution)/shard_map/all_to_all | solution.py:314
  16.7 0.0 copy-start
  16.7 3.0 %copy-done = bf16[2,4608,3,128]{3,1,2,0:T(8,128)(2,1)S(1)} copy-done((bf16[2,4608,3,128]{3,1,2,0:T(8,128)(2,1)S(1)}, bf16[2,4608,3,128]{3,1,2,0:T(8,128)(2,1)}, u32[]{:S(2)}) %copy-start) | copy-done | bytes 7077912
  19.8 2.4 %prepare.1 = (bf16[3,3456,128]{2,1,0:T(8,128)(2,1)S(1)}, bf16[3,3456,256]{2,1,0:T(8,128)(2,1)S(1)}) custom-call(s32[4]{0:T(128)S(1)} %pad_add_fusion.scalars, bf16[2,3,4608,128]{3,2,1,0:T(8,128)(2,1)S(1)} %bitcast.10), custom_call_target="tpu_custom_call" | custom-call | bytes 67108864 | tf_op jit(solution)/shard_map/prepare/pallas_call | solution.py:160
  22.2 0.0 copy-start.1
  22.2 2.4 %copy-done.1 = bf16[3,3456,256]{2,1,0:T(8,128)(2,1)} copy-done((bf16[3,3456,256]{2,1,0:T(8,128)(2,1)}, bf16[3,3456,256]{2,1,0:T(8,128)(2,1)S(1)}, u32[]{:S(2)}) %copy-start.1) | copy-done | bytes 5308440
  24.6 0.0 copy-start.3
  24.6 1.5 copy-done.3
  26.1 54.2 %all-to-all-done = bf16[5184,2,128]{2,1,0:T(2,128)(2,1)S(1)} async-done(((bf16[5184,2,128]{2,1,0:T(2,128)(2,1)}), bf16[5184,2,128]{2,1,0:T(2,128)(2,1)S(1)}, u32[]{:S(2)}, u32[]{:S(2)}) %all-to-all-start) | async-done | bytes 2654240 | tf_op jit(solution)/shard_map/all_to_all | solution.py:314
  80.3 0.0 copy-start.2
  80.3 1.9 %unpack.3.fresh_ref.refs_0_ = bf16[2,3,1152,128]{3,2,1,0:T(8,128)(2,1)} custom-call(bf16[10368,128]{1,0:T(8,128)(2,1)S(1)} %bitcast.8), custom_call_target="tpu_custom_call" | custom-call | bytes 5242880 | tf_op jit(solution)/shard_map/unpack/pallas_call | solution.py:104
  82.3 0.0 copy-start.4
  82.3 0.8 collective-permute-start.1
  83.1 0.4 unpack.2
  83.5 0.1 collective-permute-start
  83.6 0.0 copy-done.2
  83.6 0.9 copy-done.4
  84.5 23.0 %attend.1 = bf16[3456,128]{1,0:T(8,128)(2,1)} custom-call(s32[4]{0:T(128)S(1)} %pad_add_fusion.scalars, bf16[3,1152,128]{2,1,0:T(8,128)(2,1)S(1)} %bitcast.12, bf16[2,3,1152,128]{3,2,1,0:T(8,128)(2,1)} %unpack.3.fresh_ref.refs_0_, bf16[3,3456,128]{2,1,0:T(8,128)(2,1)S(1)} %copy-done.4, bf16[3,3456,256]{2,1,0:T(8,128)(2,1)S(1)} %copy-done.2), custom_call_target="tpu_custom_call" | custom-call | flops 16307453952 | bytes 16777216 | tf_op jit(solution)/shard_map/attend/pallas_call | solution.py:242
  107.6 14.1 %collective-permute-done.1.refs_2_ = bf16[2,3,1152,128]{3,2,1,0:T(8,128)(2,1)} collective-permute-done((bf16[2,3,1152,128]{3,2,1,0:T(8,128)(2,1)}, bf16[2,3,1152,128]{3,2,1,0:T(8,128)(2,1)}, u32[]{:S(2)}, u32[]{:S(2)}) %collective-permute-start.1) | collective-permute-done | bytes 1769504 | tf_op jit(solution)/shard_map/ppermute | solution.py:320
  121.6 0.0 collective-permute-start.2
  121.6 8.0 %all-to-all-start.1 = ((bf16[1728,2,128]{2,1,0:T(2,128)(2,1)}), bf16[1728,2,128]{2,1,0:T(2,128)(2,1)S(1)}, u32[]{:S(2)}, u32[]{:S(2)}) async-start(bf16[1728,2,128]{2,1,0:T(2,128)(2,1)} %bitcast.5), calls=%async_computation.1 | async-start | bytes 1769472 | tf_op jit(solution)/shard_map/all_to_all | solution.py:314
  129.7 0.0 collective-permute-done.refs_1_
  129.7 0.0 collective-permute-done.2.refs_3_
  129.7 6.6 %place.1 = bf16[2,3,4608,128]{3,2,1,0:T(8,128)(2,1)} custom-call(s32[4]{0:T(128)S(1)} %pad_add_fusion.scalars, bf16[2,3,1152,128]{3,2,1,0:T(8,128)(2,1)} %unpack.3.fresh_ref.refs_0_, bf16[2,3,1152,128]{3,2,1,0:T(8,128)(2,1)S(1)} %collective-permute-done.refs_1_, bf16[2,3,1152,128]{3,2,1,0:T(8,128)(2,1)} %collective-permute-done.1.refs_2_, ...), custom_call_target="tpu_custom_call" | custom-call | tf_op jit(solution)/shard_map/place/pallas_call | solution.py:299
  136.3 19.5 %all-to-all-done.1 = bf16[1728,2,128]{2,1,0:T(2,128)(2,1)S(1)} async-done(((bf16[1728,2,128]{2,1,0:T(2,128)(2,1)}), bf16[1728,2,128]{2,1,0:T(2,128)(2,1)S(1)}, u32[]{:S(2)}, u32[]{:S(2)}) %all-to-all-start.1) | async-done | bytes 884768 | tf_op jit(solution)/shard_map/all_to_all | solution.py:314
  155.8 1.3 merge.1
  (1 shorter events, 0.0 us)
Async XLA Ops:
  0.7 3.1 %copy-start.5 = (s32[8]{0:T(128)S(1)}, s32[8]{0:T(128)}, u32[]{:S(2)}) copy-start(s32[8]{0:T(128)} %param.5) | copy-start | bytes 100
  4.0 76.4 %all-to-all-start = ((bf16[5184,2,128]{2,1,0:T(2,128)(2,1)}), bf16[5184,2,128]{2,1,0:T(2,128)(2,1)S(1)}, u32[]{:S(2)}, u32[]{:S(2)}) async-start(bf16[5184,2,128]{2,1,0:T(2,128)(2,1)} %bitcast.13), calls=%async_computation | async-start | bytes 5308416 | tf_op jit(solution)/shard_map/all_to_all | solution.py:314
  16.7 3.0 %copy-start = (bf16[2,4608,3,128]{3,1,2,0:T(8,128)(2,1)S(1)}, bf16[2,4608,3,128]{3,1,2,0:T(8,128)(2,1)}, u32[]{:S(2)}) copy-start(bf16[2,4608,3,128]{3,1,2,0:T(8,128)(2,1)} %param.4) | copy-start | bytes 21233668
  22.2 2.4 %copy-start.1 = (bf16[3,3456,256]{2,1,0:T(8,128)(2,1)}, bf16[3,3456,256]{2,1,0:T(8,128)(2,1)S(1)}, u32[]{:S(2)}) copy-start(bf16[3,3456,256]{2,1,0:T(8,128)(2,1)S(1)} %get-tuple-element.18.old_values) | copy-start | bytes 15925252
  24.6 1.5 copy-start.3
  80.3 3.3 %copy-start.2 = (bf16[3,3456,256]{2,1,0:T(8,128)(2,1)S(1)}, bf16[3,3456,256]{2,1,0:T(8,128)(2,1)}, u32[]{:S(2)}) copy-start(bf16[3,3456,256]{2,1,0:T(8,128)(2,1)} %copy-done.1) | copy-start | bytes 15925252
  82.3 2.3 %copy-start.4 = (bf16[3,3456,128]{2,1,0:T(8,128)(2,1)S(1)}, bf16[3,3456,128]{2,1,0:T(8,128)(2,1)}, u32[]{:S(2)}) copy-start(bf16[3,3456,128]{2,1,0:T(8,128)(2,1)} %copy-done.3) | copy-start | bytes 7962628
  82.3 39.3 %collective-permute-start.1 = (bf16[2,3,1152,128]{3,2,1,0:T(8,128)(2,1)}, bf16[2,3,1152,128]{3,2,1,0:T(8,128)(2,1)}, u32[]{:S(2)}, u32[]{:S(2)}) collective-permute-start(bf16[2,3,1152,128]{3,2,1,0:T(8,128)(2,1)} %unpack.3.fresh_ref.refs_0_), channel_id=1, source_target_pairs={{0,128},{64,192},{128,0},{192,64},{1,129},{65,193},{129,1},{193,65... | collective-permute-start | bytes 5308424 | tf_op jit(solution)/shard_map/ppermute | solution.py:320
  83.5 46.2 %collective-permute-start = (bf16[2,3,1152,128]{3,2,1,0:T(8,128)(2,1)}, bf16[2,3,1152,128]{3,2,1,0:T(8,128)(2,1)S(1)}, u32[]{:S(2)}, u32[]{:S(2)}) collective-permute-start(bf16[2,3,1152,128]{3,2,1,0:T(8,128)(2,1)} %unpack.3.fresh_ref.refs_0_), channel_id=1, source_target_pairs={{0,64},{64,0},{128,192},{192,128},{1,65},{65,1},{129,193},{193,129... | collective-permute-start | bytes 5308424 | tf_op jit(solution)/shard_map/ppermute | solution.py:320
  121.6 8.1 %collective-permute-start.2 = (bf16[2,3,1152,128]{3,2,1,0:T(8,128)(2,1)}, bf16[2,3,1152,128]{3,2,1,0:T(8,128)(2,1)}, u32[]{:S(2)}, u32[]{:S(2)}) collective-permute-start(bf16[2,3,1152,128]{3,2,1,0:T(8,128)(2,1)} %collective-permute-done.1.refs_2_), channel_id=1, source_target_pairs={{0,64},{64,0},{128,192},{192,128},{1,65},{65,1},{129,193},{193,129... | collective-permute-start | bytes 5308424 | tf_op jit(solution)/shard_map/ppermute | solution.py:320
  121.6 34.2 %all-to-all-start.1 = ((bf16[1728,2,128]{2,1,0:T(2,128)(2,1)}), bf16[1728,2,128]{2,1,0:T(2,128)(2,1)S(1)}, u32[]{:S(2)}, u32[]{:S(2)}) async-start(bf16[1728,2,128]{2,1,0:T(2,128)(2,1)} %bitcast.5), calls=%async_computation.1 | async-start | bytes 1769472 | tf_op jit(solution)/shard_map/all_to_all | solution.py:314

commit v2 on v1

v2 whole, which is shorter than its diff:
```python
import functools
import math

import jax
import jax.numpy as jnp
from jax import lax
from jax.experimental import pallas as pl
from jax.experimental.pallas import tpu as pltpu
from jax.sharding import PartitionSpec as P

HEADS = 24
TXT_DEV = 2
IMG_DEV = 16
KINDS = 3
BLOCK = 384
MIB = 1024 * 1024
F32 = jnp.float32
VMEM = pl.BlockSpec(memory_space=pltpu.VMEM)
ANY = pl.BlockSpec(memory_space=pl.ANY)


def cost(mib, flops=0, exps=0):
    return pl.CostEstimate(flops=flops, bytes_accessed=mib * MIB, transcendentals=exps)


def pack_kernel(here, x_ref, o_ref, read, wide, sent, packed, in_sems, out_sems):
    kinds, tokens, pairs, _ = x_ref.shape
    steps = in_sems.shape[0]
    columns = pairs // steps
    peers = columns // here
    rows = kinds * tokens * here
    reads, writes = [], []
    for i in range(steps):
        part = pl.ds(i * columns, columns)
        copy = pltpu.make_async_copy(x_ref.at[:, :, part, :], read.at[i], in_sems.at[i])
        copy.start()
        reads.append(copy)
    for i in range(steps):
        reads[i].wait()
        wide[...] = read[i].astype(F32).reshape(wide.shape)
        for c in range(kinds):
            for t in range(tokens):
                for j in range(here):
                    first = (c * tokens + t) * columns + j
                    row = (j * kinds + c) * tokens + t
                    sent[pl.ds(row, peers, stride=rows), :] = wide[pl.ds(first, peers, stride=here), :]
        packed[i] = sent[...].astype(packed.dtype)
        part = pl.ds(i * peers * rows, peers * rows)
        copy = pltpu.make_async_copy(packed.at[i], o_ref.at[part, :], out_sems.at[i])
        copy.start()
        writes.append(copy)
    for copy in writes:
        copy.wait()


PACK_STEPS = 4


def pack(fresh_qkv, peers):
    kinds, tokens, pairs, width = fresh_qkv.shape
    columns = pairs // PACK_STEPS
    part = (kinds * tokens * columns, width)
    return pl.pallas_call(
        functools.partial(pack_kernel, pairs // peers),
        out_shape=jax.ShapeDtypeStruct((kinds * tokens * pairs, width), fresh_qkv.dtype),
        in_specs=[ANY],
        out_specs=ANY,
        scratch_shapes=[
            pltpu.VMEM((PACK_STEPS, kinds, tokens, columns, width), fresh_qkv.dtype),
            pltpu.VMEM(part, F32),
            pltpu.VMEM(part, F32),
            pltpu.VMEM((PACK_STEPS, *part), fresh_qkv.dtype),
            pltpu.SemaphoreType.DMA((PACK_STEPS,)),
            pltpu.SemaphoreType.DMA((PACK_STEPS,)),
        ],
        compiler_params=pltpu.CompilerParams(vmem_limit_bytes=60 * MIB),
        cost_estimate=cost(6),
        name="pack",
    )(fresh_qkv)


def unpack_kernel(here, x_ref, q_out, fresh_out, wide, ordered, query, both, sems):
    length = query.shape[1]
    tokens = TOKENS
    peers = length // tokens
    wide[...] = x_ref[...].astype(F32)
    copies = []
    for kinds in ((1, 2), (0,)):
        for j in range(here):
            for c in kinds:
                for t in range(tokens):
                    row = (j * KINDS + c) * tokens + t
                    block = wide[pl.ds(row, peers, stride=here * KINDS * tokens), :]
                    ordered[c, pl.ds(t, peers, stride=tokens), :] = block
            if len(kinds) == 1:
                query[j] = ordered[0].astype(query.dtype)
                copy = pltpu.make_async_copy(query.at[j], q_out.at[j], sems.at[here + j])
            else:
                both[j] = ordered[1:].astype(both.dtype)
                copy = pltpu.make_async_copy(both.at[j], fresh_out.at[j], sems.at[j])
            copy.start()
            copies.append(copy)
    for copy in copies:
        copy.wait()


TOKENS = 18


def unpack(received, here):
    total, width = received.shape
    length = total // (KINDS * here)
    dtype = received.dtype
    shapes = [(here, length, width), (here, 2, length, width)]
    return pl.pallas_call(
        functools.partial(unpack_kernel, here),
        out_shape=[jax.ShapeDtypeStruct(shape, dtype) for shape in shapes],
        in_specs=[VMEM],
        out_specs=[ANY] * len(shapes),
        scratch_shapes=[
            pltpu.VMEM((total, width), F32),
            pltpu.VMEM((KINDS, length, width), F32),
            pltpu.VMEM((here, length, width), dtype),
            pltpu.VMEM((here, 2, length, width), dtype),
            pltpu.SemaphoreType.DMA((2 * here,)),
        ],
        compiler_params=pltpu.CompilerParams(vmem_limit_bytes=12 * MIB),
        cost_estimate=cost(5),
        name="unpack",
    )(received)


def attend_kernel(text_len, tokens, scalars, q_ref, fresh_ref, stale_ref, o_ref,
                  query, keys, values, scores, highest, result, sent, sems):
    here, length, width = q_ref.shape
    total = keys.shape[1]
    groups = total // length
    peers = length // tokens
    blocks = length // BLOCK
    scale = math.log2(math.e) / math.sqrt(width)
    own = scalars[0]
    text = pl.ds(pl.multiple_of(lax.rem(groups - own, groups) * length, length), text_len)
    lanes, ones = pl.ds(0, width), pl.ds(width, width)

    def fetch(pair):
        slot = pair % 2
        new = fresh_ref.at[pair]
        pairs = [(q_ref.at[pair], query.at[slot])]
        rows = pl.ds(0, length)
        pairs += [(new.at[0], keys.at[slot, rows, :]), (new.at[1], values.at[slot, rows, lanes])]
        for step in range(1, groups):
            group = lax.rem(own + step, groups)
            source = pl.ds(pl.multiple_of(group * length, length), length)
            rows = pl.ds(step * length, length)
            pairs += [
                (stale_ref.at[0, pair, source, :], keys.at[slot, rows, :]),
                (stale_ref.at[1, pair, source, :], values.at[slot, rows, lanes]),
            ]
        copies = [
            pltpu.make_async_copy(src, dst, sems.at[slot, i]) for i, (src, dst) in enumerate(pairs)
        ]
        for copy in copies:
            copy.start()
        return copies

    def attend_pair(pair):
        slot = pair % 2
        shown = lax.broadcasted_iota(jnp.int32, (text_len, width), 0) < scalars[1 + pair]
        text_keys = keys[slot, text, :].astype(F32)
        keys[slot, text, :] = jnp.where(shown, text_keys, text_keys[0:1]).astype(keys.dtype)
        text_values = values[slot, text, lanes].astype(F32)
        values[slot, text, lanes] = jnp.where(shown, text_values, 0.0).astype(values.dtype)
        values[slot, text, ones] = jnp.where(shown, 1.0, 0.0).astype(values.dtype)

        def score(i, side):
            rows = query[slot, pl.ds(i * BLOCK, BLOCK), :]
            dims = (((1,), (1,)), ((), ()))
            found = lax.dot_general(rows, keys[slot], dims, preferred_element_type=F32)
            scores[side] = found
            top = jnp.max(found, axis=1, keepdims=True)
            highest[side] = jnp.broadcast_to(top, (BLOCK, width))

        def weigh(i, side):
            top = highest[side][:, :1]
            weights = jnp.exp2((scores[side] - top) * scale).astype(values.dtype)
            summed = jnp.dot(weights, values[slot], preferred_element_type=F32)
            result[pl.ds(i * BLOCK, BLOCK), :] = summed[:, :width] / summed[:, width:]

        score(0, 0)
        for i in range(1, blocks):
            score(i, i % 2)
            weigh(i - 1, (i - 1) % 2)
        weigh(blocks - 1, (blocks - 1) % 2)
        for t in range(tokens):
            rows = pl.ds(pair * tokens + t, peers, stride=here * tokens)
            sent[rows, :] = result[pl.ds(t, peers, stride=tokens), :]

    waiting = fetch(0)
    values[:, :, ones] = jnp.ones((2, total, width), values.dtype)
    for pair in range(here):
        for copy in waiting:
            copy.wait()
        if pair + 1 < here:
            waiting = fetch(pair + 1)
        attend_pair(pair)
    o_ref[...] = sent[...].astype(o_ref.dtype)


PAIRS = 3


def attend(scalars, query, fresh, stale, text_len, tokens):
    here, length, width = query.shape
    total = stale.shape[2]
    groups = total // length
    return pl.pallas_call(
        functools.partial(attend_kernel, text_len, tokens),
        out_shape=jax.ShapeDtypeStruct((here * length, width), query.dtype),
        in_specs=[pl.BlockSpec(memory_space=pltpu.SMEM)] + [ANY] * 3,
        out_specs=VMEM,
        scratch_shapes=[
            pltpu.VMEM((2, length, width), query.dtype),
            pltpu.VMEM((2, total, width), query.dtype),
            pltpu.VMEM((2, total, 2 * width), query.dtype),
            pltpu.VMEM((2, BLOCK, total), F32),
            pltpu.VMEM((2, BLOCK, width), F32),
            pltpu.VMEM((length, width), F32),
            pltpu.VMEM((here * length, width), F32),
            pltpu.SemaphoreType.DMA((2, 1 + 2 * groups)),
        ],
        compiler_params=pltpu.CompilerParams(vmem_limit_bytes=56 * MIB),
        cost_estimate=cost(16, 8 * here * length * total * width, here * length * total),
        name="attend",
    )(scalars, query, fresh, stale)


def merge_kernel(x_ref, o_ref, wide, spread):
    tokens, pairs, _ = o_ref.shape
    here = PAIRS
    peers = pairs // here
    wide[...] = x_ref[...].astype(F32)
    for j in range(here):
        for t in range(tokens):
            block = wide[pl.ds(j * tokens + t, peers, stride=here * tokens), :]
            spread[pl.ds(t * pairs + j, peers, stride=here), :] = block
    o_ref[...] = spread[...].reshape(o_ref.shape).astype(o_ref.dtype)


def merge(moved, pairs):
    total, width = moved.shape
    return pl.pallas_call(
        merge_kernel,
        out_shape=jax.ShapeDtypeStruct((total // pairs, pairs, width), moved.dtype),
        in_specs=[VMEM],
        out_specs=VMEM,
        scratch_shapes=[pltpu.VMEM((total, width), F32)] * 2,
        compiler_params=pltpu.CompilerParams(vmem_limit_bytes=16 * MIB),
        cost_estimate=cost(2),
        name="merge",
    )(moved)


def place_kernel(scalars, own_ref, near_ref, far_ref, *refs):
    far_near_refs, (o_ref, rows, in_sems, out_sems) = refs[:-4], refs[-4:]
    kinds, here = o_ref.shape[:2]
    length = own_ref.shape[2]
    reads, writes = [], []
    for pair in range(here):
        for kind in range(kinds):
            copies = []
            parts = [ref.at[pair, kind] for ref in (own_ref, near_ref, far_ref)]
            for step, part in enumerate(parts + [far_near_refs[pair].at[kind]]):
                group = jnp.bitwise_xor(scalars[0], step)
                at = pl.ds(pl.multiple_of(group * length, length), length)
                copy = pltpu.make_async_copy(part, rows.at[kind, pair, at, :], in_sems.at[kind, pair, step])
                copy.start()
                copies.append(copy)
            reads.append((kind, pair, copies))
    for kind, pair, copies in reads:
        for copy in copies:
            copy.wait()
        copy = pltpu.make_async_copy(rows.at[kind, pair], o_ref.at[kind, pair], out_sems.at[kind, pair])
        copy.start()
        writes.append(copy)
    for copy in writes:
        copy.wait()


def place(scalars, parts, far_near, groups):
    here, kinds, length, width = parts[0].shape
    shape = (kinds, here, groups * length, width)
    return pl.pallas_call(
        place_kernel,
        out_shape=jax.ShapeDtypeStruct(shape, parts[0].dtype),
        in_specs=[pl.BlockSpec(memory_space=pltpu.SMEM)] + [ANY] * (len(parts) + here),
        out_specs=ANY,
        scratch_shapes=[
            pltpu.VMEM(shape, parts[0].dtype),
            pltpu.SemaphoreType.DMA((kinds, here, groups)),
            pltpu.SemaphoreType.DMA((kinds, here)),
        ],
        compiler_params=pltpu.CompilerParams(vmem_limit_bytes=16 * MIB),
        cost_estimate=cost(1),
        name="place",
    )(scalars, *parts, *far_near)


def exchange(rows):
    two_rows = rows.reshape(rows.shape[0] // 2, 2, rows.shape[1])
    moved = lax.all_to_all(two_rows, "seq", split_axis=0, concat_axis=0, tiled=True)
    return moved.reshape(rows.shape)


def swap(array, bit):
    groups = lax.axis_size("patch")
    return lax.ppermute(array, "patch", [(g, g ^ bit) for g in range(groups)])


def per_device(fresh_qkv, stale_kv, text_count):
    peers = lax.axis_size("seq")
    groups = lax.axis_size("patch")
    tokens, pairs = fresh_qkv.shape[1:3]
    here = pairs // peers
    seq_len = stale_kv.shape[1]
    text_len = TXT_DEV * seq_len // (TXT_DEV + IMG_DEV)
    first_pair = lax.axis_index("seq") * here
    image_index = (first_pair + jnp.arange(here)) // HEADS
    matches = image_index[:, None] == jnp.arange(text_count.shape[0])[None, :]
    valid_counts = jnp.sum(jnp.where(matches, text_count[None, :], 0), axis=1)
    own = lax.axis_index("patch").astype(jnp.int32)
    scalars = jnp.concatenate([own[None], valid_counts.astype(jnp.int32)])
    stale = jnp.transpose(stale_kv, (0, 2, 1, 3))

    sent, scalars = lax.optimization_barrier((pack(fresh_qkv, peers), scalars))
    query, fresh = unpack(exchange(sent), here)
    far = swap(fresh, 2)
    attended = attend(scalars, query, fresh, stale, text_len, tokens)
    moved = exchange(attended)
    far, _ = lax.optimization_barrier((far, attended))
    far_near = [swap(far[pair], 1) for pair in range(here)]
    refreshed = place(scalars, [fresh, swap(fresh, 1), far], far_near, groups)
    moved, refreshed = lax.optimization_barrier((moved, refreshed))
    result = merge(moved, pairs)
    return (result, jnp.transpose(refreshed, (0, 2, 1, 3)))


def solution(mesh):
    in_specs = (P(None, ("patch", "seq"), None, None), P(None, None, "seq", None), P())
    out_specs = (P(("patch", "seq"), None, None), P(None, None, "seq", None))
    return jax.shard_map(
        per_device, mesh=mesh, in_specs=in_specs, out_specs=out_specs, check_vma=False
    )
```

time: 158 us -> 143 us (0.905)
  blocking collectives: 0 us -> 76.2 us
  waiting for transfers between devices: 87.8 us -> 20.5 us
  starting transfers between devices: 21.7 us -> 7.93 us
  local copies, waits for them, and re-layouts: 7.88 us -> 1.03 us
  Pallas kernels: 38.7 us -> 33.9 us
    all_to_all x0 -> x1, blocking collectives: none -> 76.2 us  [exchange(): lax.all_to_all(two_rows, 'seq', split_axis=0, concat_axis=0, tiled=True)]
    all_to_all x2 -> x1, waiting for transfers between devices: 73.7 us -> 3.63 us  [exchange(): lax.all_to_all(two_rows, 'seq', split_axis=0, concat_axis=0, tiled=True)]
    all_to_all x2 -> x1, starting transfers between devices: 20.8 us -> 6.43 us  [exchange(): lax.all_to_all(two_rows, 'seq', split_axis=0, concat_axis=0, tiled=True)]
    unnamed x12 -> x6, local copies, waits for them, and re-layouts: 7.88 us -> 0.92 us
    pallas_call x4 -> x2, Pallas kernels: 11.4 us -> 6.55 us  [the longest x1 4.78 us: place(): pl.pallas_call(place_kernel, out_shape=jax.ShapeDtypeStruct(shape, parts[...]
    ppermute x3 -> x5, waiting for transfers between devices: 14.1 us -> 16.9 us  [swap(): return lax.ppermute(array, 'patch', [(g, g ^ bit) for g in range(groups)])]
  transfers between devices with their start and end apart: 5 -> 6, of which waited for: 3 -> 5; matrix products, arithmetic and copies ran while one was open for 0% -> 0% of each run, Pallas kernels for 21% -> 20%
where the time goes in v2:
time: 143 us; the launch traced here: 141 us
  blocking collectives  76.2 us (53%)
  Pallas kernels  33.9 us (24%)
  waiting for transfers between devices  20.5 us (14%)
  starting transfers between devices  7.93 us (6%)
    all_to_all x1, blocking collectives, exchange(): lax.all_to_all(two_rows, 'seq', split_axis=0, concat_axis=0, tiled=True)  76.2 us
    pallas_call x1, Pallas kernels, attend(): pl.pallas_call(functools.partial(attend_kernel, text_len, tokens), out_sh...  23.1 us
    ppermute x5, waiting for transfers between devices, swap(): return lax.ppermute(array, 'patch', [(g, g ^ bit) for g in range(groups)])  16.9 us
    all_to_all x1, starting transfers between devices, exchange(): lax.all_to_all(two_rows, 'seq', split_axis=0, concat_axis=0, tiled=True)  6.43 us
    pallas_call x1, Pallas kernels, place(): pl.pallas_call(place_kernel, out_shape=jax.ShapeDtypeStruct(shape, parts[...  4.78 us
    all_to_all x1, waiting for transfers between devices, exchange(): lax.all_to_all(two_rows, 'seq', split_axis=0, concat_axis=0, tiled=True)  3.63 us
    pallas_call x1, Pallas kernels, pack(): pl.pallas_call(functools.partial(pack_kernel, pairs // peers), out_shape=...  3.02 us
  transfers between devices with their start and end apart: 6, of which 5 were waited for; matrix products, arithmetic and copies ran while one was open for 0% of the time, Pallas kernels for 20%

profile of v2, /device:TPU:4, one launch (start us, length us, event | category | flops | bytes accessed | tf_op | source)
XLA Modules:
  0.0 141.2 jit_solution(592276518283991366)
XLA Ops:
  0.7 0.0 copy-start.2
  0.7 3.0 %pack.1 = bf16[10368,128]{1,0:T(8,128)(2,1)} custom-call(bf16[3,18,192,128]{3,2,1,0:T(8,128)(2,1)} %x_ref.1), custom_call_target="tpu_custom_call" | custom-call | bytes 6291456 | tf_op jit(solution)/shard_map/pack/pallas_call | solution.py:63
  3.7 0.0 copy-done.2
  3.7 0.2 select_reduce_fusion
  3.9 0.6 pad_add_fusion.scalars
  4.5 76.2 %all_to_all.10 = bf16[5184,2,128]{2,1,0:T(2,128)(2,1)S(1)} all-to-all(bf16[5184,2,128]{2,1,0:T(2,128)(2,1)} %bitcast.15), channel_id=1, replica_groups=mesh['patch'=4,'seq'=64] {'seq'}, dimensions={0} | all-to-all | bytes 5308416 | tf_op jit(solution)/shard_map/all_to_all | solution.py:310
  80.7 1.8 %unpack.1 = (bf16[3,1152,128]{2,1,0:T(8,128)(2,1)S(1)}, bf16[3,2,1152,128]{3,2,1,0:T(8,128)(2,1)}) custom-call(bf16[10368,128]{1,0:T(8,128)(2,1)S(1)} %bitcast.13), custom_call_target="tpu_custom_call" | custom-call | bytes 5242880 | tf_op jit(solution)/shard_map/unpack/pallas_call | solution.py:115
  82.5 0.0 copy-start.1
  82.5 0.9 copy-done.1
  83.4 0.8 collective-permute-start.1
  84.2 0.0 collective-permute-start
  84.2 23.1 %attend.1 = bf16[3456,128]{1,0:T(8,128)(2,1)} custom-call(s32[4]{0:T(128)} %pad_add_fusion.scalars, bf16[3,1152,128]{2,1,0:T(8,128)(2,1)} %copy-done.1, bf16[3,2,1152,128]{3,2,1,0:T(8,128)(2,1)} %get-tuple-element.12.fresh_ref.own_ref, bf16[2,3,4608,128]{3,2,1,0:T(8,128)(2,1)} %bitcast.18), custom_call_target="tpu_custom_call" | custom-call | flops 16307453952 | bytes 16777216 | tf_op jit(solution)/shard_map/attend/pallas_call | solution.py:216
  107.3 0.0 copy-start
  107.3 6.4 %all-to-all-start.1 = ((bf16[1728,2,128]{2,1,0:T(2,128)(2,1)}), bf16[1728,2,128]{2,1,0:T(2,128)(2,1)S(1)}, u32[]{:S(2)}, u32[]{:S(2)}) async-start(bf16[1728,2,128]{2,1,0:T(2,128)(2,1)} %bitcast.17), calls=%async_computation.1 | async-start | bytes 1769472 | tf_op jit(solution)/shard_map/all_to_all | solution.py:310
  113.8 13.8 %collective-permute-done.1.far_ref = bf16[3,2,1152,128]{3,2,1,0:T(8,128)(2,1)S(1)} collective-permute-done((bf16[3,2,1152,128]{3,2,1,0:T(8,128)(2,1)}, bf16[3,2,1152,128]{3,2,1,0:T(8,128)(2,1)S(1)}, u32[]{:S(2)}, u32[]{:S(2)}) %collective-permute-start.1) | collective-permute-done | bytes 1769504 | tf_op jit(solution)/shard_map/ppermute | solution.py:316
  127.6 0.1 slice_bitcast_fusion
  127.7 0.1 collective-permute-start.4
  127.8 0.5 collective-permute-start.3
  128.3 0.1 collective-permute-start.2
  128.4 0.0 collective-permute-done.near_ref
  128.4 1.4 collective-permute-done.4.refs_2_
  129.8 0.8 collective-permute-done.3.refs_1_
  130.6 0.8 collective-permute-done.2.refs_0_
  131.5 0.0 copy-done
  131.5 4.8 %place.1 = bf16[2,3,4608,128]{3,2,1,0:T(8,128)(2,1)} custom-call(s32[4]{0:T(128)S(1)} %copy-done, bf16[3,2,1152,128]{3,2,1,0:T(8,128)(2,1)} %get-tuple-element.12.fresh_ref.own_ref, bf16[3,2,1152,128]{3,2,1,0:T(8,128)(2,1)} %collective-permute-done.near_ref, bf16[3,2,1152,128]{3,2,1,0:T(8,128)(2,1)S(1)} %collective-permute-done.1.far_ref, ...), custom_call_target="tpu_custom_call" | custom-call | bytes 1048576 | tf_op jit(solution)/shard_map/place/pallas_call | solution.py:292
  136.3 3.6 %all-to-all-done.1 = bf16[1728,2,128]{2,1,0:T(2,128)(2,1)S(1)} async-done(((bf16[1728,2,128]{2,1,0:T(2,128)(2,1)}), bf16[1728,2,128]{2,1,0:T(2,128)(2,1)S(1)}, u32[]{:S(2)}, u32[]{:S(2)}) %all-to-all-start.1) | async-done | bytes 884768 | tf_op jit(solution)/shard_map/all_to_all | solution.py:310
  139.9 1.3 merge.1
  (1 shorter events, 0.0 us)
Async XLA Ops:
  0.7 3.0 %copy-start.2 = (s32[8]{0:T(128)S(1)}, s32[8]{0:T(128)}, u32[]{:S(2)}) copy-start(s32[8]{0:T(128)} %param.5) | copy-start | bytes 100
  82.5 0.9 copy-start.1
  83.4 44.2 %collective-permute-start.1 = (bf16[3,2,1152,128]{3,2,1,0:T(8,128)(2,1)}, bf16[3,2,1152,128]{3,2,1,0:T(8,128)(2,1)S(1)}, u32[]{:S(2)}, u32[]{:S(2)}) collective-permute-start(bf16[3,2,1152,128]{3,2,1,0:T(8,128)(2,1)} %get-tuple-element.12.fresh_ref.own_ref), channel_id=1, source_target_pairs={{0,128},{64,192},{128,0},{192,64},{1,129},{65,193},{129,1},{193,65... | collective-permute-start | bytes 5308424 | tf_op jit(solution)/shard_map/ppermute | solution.py:316
  84.2 44.2 %collective-permute-start = (bf16[3,2,1152,128]{3,2,1,0:T(8,128)(2,1)}, bf16[3,2,1152,128]{3,2,1,0:T(8,128)(2,1)}, u32[]{:S(2)}, u32[]{:S(2)}) collective-permute-start(bf16[3,2,1152,128]{3,2,1,0:T(8,128)(2,1)} %get-tuple-element.12.fresh_ref.own_ref), channel_id=1, source_target_pairs={{0,64},{64,0},{128,192},{192,128},{1,65},{65,1},{129,193},{193,129... | collective-permute-start | bytes 5308424 | tf_op jit(solution)/shard_map/ppermute | solution.py:316
  107.3 24.2 %copy-start = (s32[4]{0:T(128)S(1)}, s32[4]{0:T(128)}, u32[]{:S(2)}) copy-start(s32[4]{0:T(128)} %pad_add_fusion.scalars) | copy-start | bytes 52
  107.3 32.6 %all-to-all-start.1 = ((bf16[1728,2,128]{2,1,0:T(2,128)(2,1)}), bf16[1728,2,128]{2,1,0:T(2,128)(2,1)S(1)}, u32[]{:S(2)}, u32[]{:S(2)}) async-start(bf16[1728,2,128]{2,1,0:T(2,128)(2,1)} %bitcast.17), calls=%async_computation.1 | async-start | bytes 1769472 | tf_op jit(solution)/shard_map/all_to_all | solution.py:310
  127.7 2.1 %collective-permute-start.4 = (bf16[2,1152,128]{2,1,0:T(8,128)(2,1)S(1)}, bf16[2,1152,128]{2,1,0:T(8,128)(2,1)S(1)}, u32[]{:S(2)}, u32[]{:S(2)}) collective-permute-start(bf16[2,1152,128]{2,1,0:T(8,128)(2,1)S(1)} %get-tuple-element.16), channel_id=1, source_target_pairs={{0,64},{64,0},{128,192},{192,128},{1,65},{65,1},{129,193},{193,129... | collective-permute-start | bytes 1769480 | tf_op jit(solution)/shard_map/ppermute | solution.py:316
  127.8 2.8 %collective-permute-start.3 = (bf16[2,1152,128]{2,1,0:T(8,128)(2,1)S(1)}, bf16[2,1152,128]{2,1,0:T(8,128)(2,1)S(1)}, u32[]{:S(2)}, u32[]{:S(2)}) collective-permute-start(bf16[2,1152,128]{2,1,0:T(8,128)(2,1)S(1)} %get-tuple-element.17), channel_id=1, source_target_pairs={{0,64},{64,0},{128,192},{192,128},{1,65},{65,1},{129,193},{193,129... | collective-permute-start | bytes 1769480 | tf_op jit(solution)/shard_map/ppermute | solution.py:316
  128.3 3.2 %collective-permute-start.2 = (bf16[2,1152,128]{2,1,0:T(8,128)(2,1)S(1)}, bf16[2,1152,128]{2,1,0:T(8,128)(2,1)S(1)}, u32[]{:S(2)}, u32[]{:S(2)}) collective-permute-start(bf16[2,1152,128]{2,1,0:T(8,128)(2,1)S(1)} %get-tuple-element.18), channel_id=1, source_target_pairs={{0,64},{64,0},{128,192},{192,128},{1,65},{65,1},{129,193},{193,129... | collective-permute-start | bytes 1769480 | tf_op jit(solution)/shard_map/ppermute | solution.py:316

commit v3 on v2

v3 whole, which is shorter than its diff:
```python
import functools
import math

import jax
import jax.numpy as jnp
from jax import lax
from jax.experimental import pallas as pl
from jax.experimental.pallas import tpu as pltpu
from jax.sharding import PartitionSpec as P

HEADS = 24
TXT_DEV = 2
IMG_DEV = 16
KINDS = 3
PAIRS = 3
BLOCK = 576
MIB = 1024 * 1024
F32 = jnp.float32
VMEM = pl.BlockSpec(memory_space=pltpu.VMEM)
ANY = pl.BlockSpec(memory_space=pl.ANY)
HBM = pl.BlockSpec(memory_space=pltpu.HBM)


def cost(mib, flops=0, exps=0):
    return pl.CostEstimate(flops=flops, bytes_accessed=mib * MIB, transcendentals=exps)


def pack_kernel(here, chosen, x_ref, o_ref, read, wide, sent, packed, in_sems, out_sems):
    kinds, tokens, pairs, _ = x_ref.shape
    steps = in_sems.shape[0]
    columns = pairs // steps
    peers = columns // here
    rows = kinds * tokens * len(chosen)
    reads, writes = [], []
    for i in range(steps):
        part = pl.ds(i * columns, columns)
        copy = pltpu.make_async_copy(x_ref.at[:, :, part, :], read.at[i], in_sems.at[i])
        copy.start()
        reads.append(copy)
    for i in range(steps):
        reads[i].wait()
        wide[...] = read[i].astype(F32).reshape(wide.shape)
        for c in range(kinds):
            for t in range(tokens):
                for n, j in enumerate(chosen):
                    first = (c * tokens + t) * columns + j
                    row = (n * kinds + c) * tokens + t
                    sent[pl.ds(row, peers, stride=rows), :] = wide[pl.ds(first, peers, stride=here), :]
        packed[i] = sent[...].astype(packed.dtype)
        part = pl.ds(i * peers * rows, peers * rows)
        copy = pltpu.make_async_copy(packed.at[i], o_ref.at[part, :], out_sems.at[i])
        copy.start()
        writes.append(copy)
    for copy in writes:
        copy.wait()


PACK_STEPS = 4


def pack(fresh_qkv, peers, chosen):
    kinds, tokens, pairs, width = fresh_qkv.shape
    here = pairs // peers
    columns = pairs // PACK_STEPS
    rows = kinds * tokens * len(chosen)
    part = (rows * columns // here, width)
    return pl.pallas_call(
        functools.partial(pack_kernel, here, chosen),
        out_shape=jax.ShapeDtypeStruct((rows * peers, width), fresh_qkv.dtype),
        in_specs=[ANY],
        out_specs=ANY,
        scratch_shapes=[
            pltpu.VMEM((PACK_STEPS, kinds, tokens, columns, width), fresh_qkv.dtype),
            pltpu.VMEM((kinds * tokens * columns, width), F32),
            pltpu.VMEM(part, F32),
            pltpu.VMEM((PACK_STEPS, *part), fresh_qkv.dtype),
            pltpu.SemaphoreType.DMA((PACK_STEPS,)),
            pltpu.SemaphoreType.DMA((PACK_STEPS,)),
        ],
        compiler_params=pltpu.CompilerParams(vmem_limit_bytes=60 * MIB),
        cost_estimate=cost(6),
        name="pack",
    )(fresh_qkv)


def unpack_kernel(here, x_ref, q_ref, fresh_out, wide, ordered, both, sems):
    length = q_ref.shape[1]
    tokens = TOKENS
    peers = length // tokens
    wide[...] = x_ref[...].astype(F32)
    copies = []
    for kinds in ((1, 2), (0,)):
        for j in range(here):
            for c in kinds:
                for t in range(tokens):
                    row = (j * KINDS + c) * tokens + t
                    block = wide[pl.ds(row, peers, stride=here * KINDS * tokens), :]
                    ordered[c, pl.ds(t, peers, stride=tokens), :] = block
            if len(kinds) == 1:
                q_ref[j] = ordered[0].astype(q_ref.dtype)
            else:
                both[j] = ordered[1:].astype(both.dtype)
                copy = pltpu.make_async_copy(both.at[j], fresh_out.at[j], sems.at[j])
                copy.start()
                copies.append(copy)
    for copy in copies:
        copy.wait()


TOKENS = 18


def unpack(received, here):
    total, width = received.shape
    length = total // (KINDS * here)
    dtype = received.dtype
    shapes = [(here, length, width), (here, 2, length, width)]
    return pl.pallas_call(
        functools.partial(unpack_kernel, here),
        out_shape=[jax.ShapeDtypeStruct(shape, dtype) for shape in shapes],
        in_specs=[VMEM],
        out_specs=[VMEM, HBM],
        scratch_shapes=[
            pltpu.VMEM((total, width), F32),
            pltpu.VMEM((KINDS, length, width), F32),
            pltpu.VMEM((here, 2, length, width), dtype),
            pltpu.SemaphoreType.DMA((here,)),
        ],
        compiler_params=pltpu.CompilerParams(vmem_limit_bytes=16 * MIB),
        cost_estimate=cost(5),
        name="unpack",
    )(received)


def attend_kernel(text_len, tokens, first_pair, here, counts, q_ref, fresh_ref, stale_ref, done_ref, o_ref,
                  keys, values, scores, result, done, sent, sems, done_sem):
    count, length, width = q_ref.shape
    total = keys.shape[1]
    groups = total // length
    peers = length // tokens
    blocks = length // BLOCK
    scale = math.log2(math.e) / math.sqrt(width)
    last = first_pair + count == here
    own = lax.axis_index("patch").astype(jnp.int32)
    own_pair = lax.axis_index("seq").astype(jnp.int32) * here + first_pair
    text = pl.ds(pl.multiple_of(lax.rem(groups - own, groups) * length, length), text_len)
    lanes, ones = pl.ds(0, width), pl.ds(width, width)

    def fetch(pair):
        slot = pair % 2
        rows = pl.ds(0, length)
        pairs = [
            (fresh_ref.at[pair, 0], keys.at[slot, rows, :]),
            (fresh_ref.at[pair, 1], values.at[slot, rows, lanes]),
        ]
        for step in range(1, groups):
            group = lax.rem(own + step, groups)
            source = pl.ds(pl.multiple_of(group * length, length), length)
            rows = pl.ds(step * length, length)
            pairs += [
                (stale_ref.at[0, first_pair + pair, source, :], keys.at[slot, rows, :]),
                (stale_ref.at[1, first_pair + pair, source, :], values.at[slot, rows, lanes]),
            ]
        copies = [
            pltpu.make_async_copy(src, dst, sems.at[slot, i]) for i, (src, dst) in enumerate(pairs)
        ]
        for copy in copies:
            copy.start()
        return copies

    def lay_out(pair, source):
        for t in range(tokens):
            rows = pl.ds(pair * tokens + t, peers, stride=here * tokens)
            sent[rows, :] = source[pl.ds(t, peers, stride=tokens), :]

    def attend_pair(pair):
        slot = pair % 2
        valid = counts[(own_pair + pair) // HEADS]
        shown = lax.broadcasted_iota(jnp.int32, (text_len, width), 0) < valid
        text_keys = keys[slot, text, :].astype(F32)
        keys[slot, text, :] = jnp.where(shown, text_keys, text_keys[0:1]).astype(keys.dtype)
        text_values = values[slot, text, lanes].astype(F32)
        values[slot, text, lanes] = jnp.where(shown, text_values, 0.0).astype(values.dtype)
        values[slot, text, ones] = jnp.where(shown, 1.0, 0.0).astype(values.dtype)

        def score(i, side):
            rows = q_ref[pair, pl.ds(i * BLOCK, BLOCK), :]
            dims = (((1,), (1,)), ((), ()))
            top = None
            for at in range(0, total, CHUNK):
                part = keys[slot, pl.ds(at, CHUNK), :]
                found = lax.dot_general(rows, part, dims, preferred_element_type=F32)
                scores[side, :, pl.ds(at, CHUNK)] = found
                for lane in range(0, CHUNK, width):
                    piece = found[:, lane:lane + width]
                    top = piece if top is None else jnp.maximum(top, piece)
            return jnp.max(top, axis=1, keepdims=True)

        def weigh(i, side, top):
            summed = None
            for at in range(0, total, CHUNK):
                part = pl.ds(at, CHUNK)
                weights = jnp.exp2((scores[side, :, part] - top) * scale).astype(values.dtype)
                term = jnp.dot(weights, values[slot, part, :], preferred_element_type=F32)
                summed = term if summed is None else summed + term
            result[pl.ds(i * BLOCK, BLOCK), :] = summed[:, :width] / summed[:, width:]

        top = score(0, 0)
        for i in range(1, blocks):
            new_top = score(i, i % 2)
            weigh(i - 1, (i - 1) % 2, top)
            top = new_top
        weigh(blocks - 1, (blocks - 1) % 2, top)

    waiting = fetch(0)
    values[:, :, ones] = jnp.ones((2, total, width), values.dtype)
    if first_pair:
        earlier = pltpu.make_async_copy(done_ref, done, done_sem)
        earlier.start()
    for pair in range(count):
        for copy in waiting:
            copy.wait()
        if pair + 1 < count:
            waiting = fetch(pair + 1)
        attend_pair(pair)
        if last:
            lay_out(first_pair + pair, result)
        else:
            o_ref[pair] = result[...]
    if last:
        if first_pair:
            earlier.wait()
        for pair in range(first_pair):
            lay_out(pair, done.at[pair])
        o_ref[...] = sent[...].astype(o_ref.dtype)


CHUNK = 512


def attend(counts, query, fresh, stale, done, first_pair, text_len, tokens):
    count, length, width = query.shape
    here, total = stale.shape[1:3]
    groups = total // length
    last = first_pair + count == here
    if last:
        out_shape = jax.ShapeDtypeStruct((here * length, width), query.dtype)
    else:
        out_shape = jax.ShapeDtypeStruct(query.shape, F32)
    done = counts
    return pl.pallas_call(
        functools.partial(attend_kernel, text_len, tokens, first_pair, here),
        out_shape=out_shape,
        in_specs=[pl.BlockSpec(memory_space=pltpu.SMEM), VMEM, HBM, HBM, ANY],
        out_specs=VMEM,
        scratch_shapes=[
            pltpu.VMEM((2, total, width), query.dtype),
            pltpu.VMEM((2, total, 2 * width), query.dtype),
            pltpu.VMEM((2, BLOCK, total), F32),
            pltpu.VMEM((length, width), F32),
            pltpu.VMEM(done.shape, done.dtype),
            pltpu.VMEM((here * length, width), F32),
            pltpu.SemaphoreType.DMA((2, 2 * groups)),
            pltpu.SemaphoreType.DMA,
        ],
        compiler_params=pltpu.CompilerParams(vmem_limit_bytes=36 * MIB),
        cost_estimate=cost(16, 8 * count * length * total * width, count * length * total),
        name="attend",
    )(counts, query, fresh, stale, done)


def merge_kernel(x_ref, o_ref, wide, spread):
    tokens, pairs, _ = o_ref.shape
    here = PAIRS
    peers = pairs // here
    wide[...] = x_ref[...].astype(F32)
    for j in range(here):
        for t in range(tokens):
            block = wide[pl.ds(j * tokens + t, peers, stride=here * tokens), :]
            spread[pl.ds(t * pairs + j, peers, stride=here), :] = block
    o_ref[...] = spread[...].reshape(o_ref.shape).astype(o_ref.dtype)


def merge(moved, pairs):
    total, width = moved.shape
    return pl.pallas_call(
        merge_kernel,
        out_shape=jax.ShapeDtypeStruct((total // pairs, pairs, width), moved.dtype),
        in_specs=[VMEM],
        out_specs=VMEM,
        scratch_shapes=[pltpu.VMEM((total, width), F32)] * 2,
        compiler_params=pltpu.CompilerParams(vmem_limit_bytes=16 * MIB),
        cost_estimate=cost(2),
        name="merge",
    )(moved)


def place_kernel(groups, *refs):
    part_refs, (o_ref, rows, in_sems, out_sems) = refs[:-4], refs[-4:]
    kinds, here = o_ref.shape[:2]
    length = o_ref.shape[2] // groups
    own = lax.axis_index("patch").astype(jnp.int32)
    sources = [[ref.at[pair] for pair in range(here)] for ref in part_refs[: groups - 1]]
    sources.append([ref.at[0] for ref in part_refs[groups - 1 :]])
    reads, writes = [], []
    for pair in range(here):
        for kind in range(kinds):
            copies = []
            for step in range(groups):
                group = jnp.bitwise_xor(own, step)
                at = pl.ds(pl.multiple_of(group * length, length), length)
                copy = pltpu.make_async_copy(
                    sources[step][pair].at[kind], rows.at[kind, pair, at, :], in_sems.at[kind, pair, step]
                )
                copy.start()
                copies.append(copy)
            reads.append((kind, pair, copies))
    for kind, pair, copies in reads:
        for copy in copies:
            copy.wait()
        copy = pltpu.make_async_copy(rows.at[kind, pair], o_ref.at[kind, pair], out_sems.at[kind, pair])
        copy.start()
        writes.append(copy)
    for copy in writes:
        copy.wait()


def place(parts, far_near, here, groups):
    _, kinds, length, width = parts[0].shape
    shape = (kinds, here, groups * length, width)
    return pl.pallas_call(
        functools.partial(place_kernel, groups),
        out_shape=jax.ShapeDtypeStruct(shape, parts[0].dtype),
        in_specs=[ANY] * (len(parts) + here),
        out_specs=ANY,
        scratch_shapes=[
            pltpu.VMEM(shape, parts[0].dtype),
            pltpu.SemaphoreType.DMA((kinds, here, groups)),
            pltpu.SemaphoreType.DMA((kinds, here)),
        ],
        compiler_params=pltpu.CompilerParams(vmem_limit_bytes=16 * MIB),
        cost_estimate=cost(1),
        name="place",
    )(*parts, *far_near)


def exchange(rows):
    two_rows = rows.reshape(rows.shape[0] // 2, 2, rows.shape[1])
    moved = lax.all_to_all(two_rows, "seq", split_axis=0, concat_axis=0, tiled=True)
    return moved.reshape(rows.shape)


def swap(array, bit):
    groups = lax.axis_size("patch")
    return lax.ppermute(array, "patch", [(g, g ^ bit) for g in range(groups)])


def per_device(fresh_qkv, stale_kv, text_count):
    peers = lax.axis_size("seq")
    groups = lax.axis_size("patch")
    tokens, pairs = fresh_qkv.shape[1:3]
    here = pairs // peers
    seq_len = stale_kv.shape[1]
    text_len = TXT_DEV * seq_len // (TXT_DEV + IMG_DEV)
    stale = jnp.transpose(stale_kv, (0, 2, 1, 3))

    every = tuple(range(here))
    query, fresh = unpack(exchange(pack(fresh_qkv, peers, every)), here)
    far = swap(fresh, 2)
    attended = attend(text_count, query, fresh, stale, None, 0, text_len, tokens)
    moved = exchange(attended)
    far, _ = lax.optimization_barrier((far, attended))
    far_near = [swap(far[pair : pair + 1], 1) for pair in range(here)]
    refreshed = place([fresh, swap(fresh, 1), far], far_near, here, groups)
    moved, refreshed = lax.optimization_barrier((moved, refreshed))
    result = merge(moved, pairs)
    return (result, jnp.transpose(refreshed, (0, 2, 1, 3)))


def solution(mesh):
    in_specs = (P(None, ("patch", "seq"), None, None), P(None, None, "seq", None), P())
    out_specs = (P(("patch", "seq"), None, None), P(None, None, "seq", None))
    return jax.shard_map(
        per_device, mesh=mesh, in_specs=in_specs, out_specs=out_specs, check_vma=False
    )
```

time: 143 us -> 139 us (0.972)
  Pallas kernels: 33.9 us -> 31.6 us
    ppermute x5, waiting for transfers between devices: 16.9 us -> 20.3 us  [swap(): return lax.ppermute(array, 'patch', [(g, g ^ bit) for g in range(groups)])]
    all_to_all x1, waiting for transfers between devices: 3.63 us -> 0.77 us  [exchange(): lax.all_to_all(two_rows, 'seq', split_axis=0, concat_axis=0, tiled=True)]
    pallas_call x3, Pallas kernels: 30.9 us -> 28.6 us  [the longest x1 21.3 us: attend(): pl.pallas_call(functools.partial(attend_kernel, text_len, tokens, first_p...]
  transfers between devices with their start and end apart: 6 -> 6, of which waited for: 5 -> 5; matrix products, arithmetic and copies ran while one was open for 0% -> 0% of each run, Pallas kernels for 20% -> 19%
where the time goes in v3:
time: 139 us; the launch traced here: 138 us
  blocking collectives  76.5 us (55%)
  Pallas kernels  31.6 us (23%)
  waiting for transfers between devices  21.1 us (15%)
  starting transfers between devices  8.01 us (6%)
    all_to_all x1, blocking collectives, exchange(): lax.all_to_all(two_rows, 'seq', split_axis=0, concat_axis=0, tiled=True)  76.5 us
    pallas_call x1, Pallas kernels, attend(): pl.pallas_call(functools.partial(attend_kernel, text_len, tokens, first_p...  21.3 us
    ppermute x5, waiting for transfers between devices, swap(): return lax.ppermute(array, 'patch', [(g, g ^ bit) for g in range(groups)])  20.3 us
    all_to_all x1, starting transfers between devices, exchange(): lax.all_to_all(two_rows, 'seq', split_axis=0, concat_axis=0, tiled=True)  6.43 us
    pallas_call x1, Pallas kernels, place(): pl.pallas_call(functools.partial(place_kernel, groups), out_shape=jax.Sha...  4.24 us
    pallas_call x1, Pallas kernels, pack(): pl.pallas_call(functools.partial(pack_kernel, here, chosen), out_shape=ja...  3.01 us
  transfers between devices with their start and end apart: 6, of which 5 were waited for; matrix products, arithmetic and copies ran while one was open for 0% of the time, Pallas kernels for 19%

profile of v3, /device:TPU:4, one launch (start us, length us, event | category | flops | bytes accessed | tf_op | source)
XLA Modules:
  0.0 138.0 jit_solution(10974426511706381854)
XLA Ops:
  0.6 3.0 %pack.1 = bf16[10368,128]{1,0:T(8,128)(2,1)} custom-call(bf16[3,18,192,128]{3,2,1,0:T(8,128)(2,1)} %x_ref.1), custom_call_target="tpu_custom_call" | custom-call | bytes 6291456 | tf_op jit(solution)/shard_map/pack/pallas_call | solution.py:67
  3.6 0.0 copy-start
  3.7 76.5 %all_to_all.10 = bf16[5184,2,128]{2,1,0:T(2,128)(2,1)S(1)} all-to-all(bf16[5184,2,128]{2,1,0:T(2,128)(2,1)} %bitcast.9), channel_id=1, replica_groups=mesh['patch'=4,'seq'=64] {'seq'}, dimensions={0} | all-to-all | bytes 5308416 | tf_op jit(solution)/shard_map/all_to_all | solution.py:349
  80.2 0.0 copy-start.1
  80.2 1.7 %unpack.1 = (bf16[3,1152,128]{2,1,0:T(8,128)(2,1)S(1)}, bf16[3,2,1152,128]{3,2,1,0:T(8,128)(2,1)}) custom-call(bf16[10368,128]{1,0:T(8,128)(2,1)S(1)} %bitcast.6), custom_call_target="tpu_custom_call" | custom-call | bytes 5242880 | tf_op jit(solution)/shard_map/unpack/pallas_call | solution.py:118
  81.9 0.9 collective-permute-start.1
  82.8 0.0 collective-permute-start
  82.8 0.0 copy-done
  82.8 0.0 copy-done.1
  82.8 21.3 %attend.1 = bf16[3456,128]{1,0:T(8,128)(2,1)} custom-call(s32[8]{0:T(128)S(1)} %copy-done.1, bf16[3,1152,128]{2,1,0:T(8,128)(2,1)S(1)} %get-tuple-element.7.q_ref, bf16[3,2,1152,128]{3,2,1,0:T(8,128)(2,1)} %get-tuple-element.8.fresh_ref.refs_0_, bf16[2,3,4608,128]{3,2,1,0:T(8,128)(2,1)S(1)} %bitcast.8, s32[8]{0:T(128)S(1)} %copy-done.1), custom_call_target="tpu_custom_call" | custom-call | flops 16307453952 | bytes 16777216 | tf_op jit(solution)/shard_map/attend/pallas_call | solution.py:251
  104.1 6.4 %all-to-all-start.1 = ((bf16[1728,2,128]{2,1,0:T(2,128)(2,1)}), bf16[1728,2,128]{2,1,0:T(2,128)(2,1)S(1)}, u32[]{:S(2)}, u32[]{:S(2)}) async-start(bf16[1728,2,128]{2,1,0:T(2,128)(2,1)} %bitcast.3), calls=%async_computation.1 | async-start | bytes 1769472 | tf_op jit(solution)/shard_map/all_to_all | solution.py:349
  110.6 17.2 %collective-permute-done.1.refs_2_ = bf16[3,2,1152,128]{3,2,1,0:T(8,128)(2,1)S(1)} collective-permute-done((bf16[3,2,1152,128]{3,2,1,0:T(8,128)(2,1)}, bf16[3,2,1152,128]{3,2,1,0:T(8,128)(2,1)S(1)}, u32[]{:S(2)}, u32[]{:S(2)}) %collective-permute-start.1) | collective-permute-done | bytes 1769504 | tf_op jit(solution)/shard_map/ppermute | solution.py:355
  127.8 0.1 fusion
  127.9 0.1 collective-permute-start.4
  128.0 0.5 collective-permute-start.3
  128.5 0.1 collective-permute-start.2
  128.6 0.0 collective-permute-done.refs_1_
  128.6 1.4 %collective-permute-done.4.refs_5_ = bf16[1,2,1152,128]{3,2,1,0:T(8,128)(2,1)S(1)} collective-permute-done((bf16[1,2,1152,128]{3,2,1,0:T(8,128)(2,1)S(1)}, bf16[1,2,1152,128]{3,2,1,0:T(8,128)(2,1)S(1)}, u32[]{:S(2)}, u32[]{:S(2)}) %collective-permute-start.4) | collective-permute-done | bytes 589856 | tf_op jit(solution)/shard_map/ppermute | solution.py:355
  130.0 0.8 collective-permute-done.3.refs_4_
  130.8 0.8 collective-permute-done.2.refs_3_
  131.7 4.2 %place.1 = bf16[2,3,4608,128]{3,2,1,0:T(8,128)(2,1)} custom-call(bf16[3,2,1152,128]{3,2,1,0:T(8,128)(2,1)} %get-tuple-element.8.fresh_ref.refs_0_, bf16[3,2,1152,128]{3,2,1,0:T(8,128)(2,1)} %collective-permute-done.refs_1_, bf16[3,2,1152,128]{3,2,1,0:T(8,128)(2,1)S(1)} %collective-permute-done.1.refs_2_, ...), custom_call_target="tpu_custom_call" | custom-call | bytes 1048576 | tf_op jit(solution)/shard_map/place/pallas_call | solution.py:331
  135.9 0.8 all-to-all-done.1
  136.7 1.3 merge.1
Async XLA Ops:
  3.6 79.1 %copy-start = (bf16[2,4608,3,128]{3,1,2,0:T(8,128)(2,1)S(1)}, bf16[2,4608,3,128]{3,1,2,0:T(8,128)(2,1)}, u32[]{:S(2)}) copy-start(bf16[2,4608,3,128]{3,1,2,0:T(8,128)(2,1)} %param.4) | copy-start | bytes 21233668
  80.2 2.6 %copy-start.1 = (s32[8]{0:T(128)S(1)}, s32[8]{0:T(128)}, u32[]{:S(2)}) copy-start(s32[8]{0:T(128)} %done_ref.1) | copy-start | bytes 100
  81.9 45.9 %collective-permute-start.1 = (bf16[3,2,1152,128]{3,2,1,0:T(8,128)(2,1)}, bf16[3,2,1152,128]{3,2,1,0:T(8,128)(2,1)S(1)}, u32[]{:S(2)}, u32[]{:S(2)}) collective-permute-start(bf16[3,2,1152,128]{3,2,1,0:T(8,128)(2,1)} %get-tuple-element.8.fresh_ref.refs_0_), channel_id=1, source_target_pairs={{0,128},{64,192},{128,0},{192,64},{1,129},{65,193},{129,1},{193,65... | collective-permute-start | bytes 5308424 | tf_op jit(solution)/shard_map/ppermute | solution.py:355
  82.8 45.8 %collective-permute-start = (bf16[3,2,1152,128]{3,2,1,0:T(8,128)(2,1)}, bf16[3,2,1152,128]{3,2,1,0:T(8,128)(2,1)}, u32[]{:S(2)}, u32[]{:S(2)}) collective-permute-start(bf16[3,2,1152,128]{3,2,1,0:T(8,128)(2,1)} %get-tuple-element.8.fresh_ref.refs_0_), channel_id=1, source_target_pairs={{0,64},{64,0},{128,192},{192,128},{1,65},{65,1},{129,193},{193,129... | collective-permute-start | bytes 5308424 | tf_op jit(solution)/shard_map/ppermute | solution.py:355
  104.1 32.6 %all-to-all-start.1 = ((bf16[1728,2,128]{2,1,0:T(2,128)(2,1)}), bf16[1728,2,128]{2,1,0:T(2,128)(2,1)S(1)}, u32[]{:S(2)}, u32[]{:S(2)}) async-start(bf16[1728,2,128]{2,1,0:T(2,128)(2,1)} %bitcast.3), calls=%async_computation.1 | async-start | bytes 1769472 | tf_op jit(solution)/shard_map/all_to_all | solution.py:349
  127.9 2.1 %collective-permute-start.4 = (bf16[1,2,1152,128]{3,2,1,0:T(8,128)(2,1)S(1)}, bf16[1,2,1152,128]{3,2,1,0:T(8,128)(2,1)S(1)}, u32[]{:S(2)}, u32[]{:S(2)}) collective-permute-start(bf16[1,2,1152,128]{3,2,1,0:T(8,128)(2,1)S(1)} %get-tuple-element.12), channel_id=1, source_target_pairs={{0,64},{64,0},{128,192},{192,128},{1,65},{65,1},{129,193},{193,129... | collective-permute-start | bytes 1769480 | tf_op jit(solution)/shard_map/ppermute | solution.py:355
  128.0 2.8 %collective-permute-start.3 = (bf16[1,2,1152,128]{3,2,1,0:T(8,128)(2,1)S(1)}, bf16[1,2,1152,128]{3,2,1,0:T(8,128)(2,1)S(1)}, u32[]{:S(2)}, u32[]{:S(2)}) collective-permute-start(bf16[1,2,1152,128]{3,2,1,0:T(8,128)(2,1)S(1)} %get-tuple-element.13), channel_id=1, source_target_pairs={{0,64},{64,0},{128,192},{192,128},{1,65},{65,1},{129,193},{193,129... | collective-permute-start | bytes 1769480 | tf_op jit(solution)/shard_map/ppermute | solution.py:355
  128.5 3.2 %collective-permute-start.2 = (bf16[1,2,1152,128]{3,2,1,0:T(8,128)(2,1)S(1)}, bf16[1,2,1152,128]{3,2,1,0:T(8,128)(2,1)S(1)}, u32[]{:S(2)}, u32[]{:S(2)}) collective-permute-start(bf16[1,2,1152,128]{3,2,1,0:T(8,128)(2,1)S(1)} %get-tuple-element.14), channel_id=1, source_target_pairs={{0,64},{64,0},{128,192},{192,128},{1,65},{65,1},{129,193},{193,129... | collective-permute-start | bytes 1769480 | tf_op jit(solution)/shard_map/ppermute | solution.py:355

commit v4 on v3

--- a/solution.py
+++ b/solution.py
@@ -25,12 +25,12 @@
     return pl.CostEstimate(flops=flops, bytes_accessed=mib * MIB, transcendentals=exps)
 
 
-def pack_kernel(here, chosen, x_ref, o_ref, read, wide, sent, packed, in_sems, out_sems):
+def pack_kernel(here, runs, x_ref, *refs):
+    o_refs, (read, wide, sent, packed, in_sems, out_sems) = refs[: len(runs)], refs[len(runs) :]
     kinds, tokens, pairs, _ = x_ref.shape
     steps = in_sems.shape[0]
     columns = pairs // steps
     peers = columns // here
-    rows = kinds * tokens * len(chosen)
     reads, writes = [], []
     for i in range(steps):
         part = pl.ds(i * columns, columns)
@@ -40,17 +40,25 @@
     for i in range(steps):
         reads[i].wait()
         wide[...] = read[i].astype(F32).reshape(wide.shape)
-        for c in range(kinds):
-            for t in range(tokens):
-                for n, j in enumerate(chosen):
-                    first = (c * tokens + t) * columns + j
-                    row = (n * kinds + c) * tokens + t
-                    sent[pl.ds(row, peers, stride=rows), :] = wide[pl.ds(first, peers, stride=here), :]
-        packed[i] = sent[...].astype(packed.dtype)
-        part = pl.ds(i * peers * rows, peers * rows)
-        copy = pltpu.make_async_copy(packed.at[i], o_ref.at[part, :], out_sems.at[i])
-        copy.start()
-        writes.append(copy)
+        base = 0
+        for k, run in enumerate(runs):
+            rows = kinds * tokens * len(run)
+            length = peers * rows
+            for c in range(kinds):
+                for t in range(tokens):
+                    for n, j in enumerate(run):
+                        first = (c * tokens + t) * columns + j
+                        row = base + (n * kinds + c) * tokens + t
+                        block = wide[pl.ds(first, peers, stride=here), :]
+                        sent[pl.ds(row, peers, stride=rows), :] = block
+            part = pl.ds(base, length)
+            packed[i, part, :] = sent[part, :].astype(packed.dtype)
+            copy = pltpu.make_async_copy(
+                packed.at[i, part, :], o_refs[k].at[pl.ds(i * length, length), :], out_sems.at[i, k]
+            )
+            copy.start()
+            writes.append(copy)
+            base += length
     for copy in writes:
         copy.wait()
 
@@ -58,24 +66,24 @@
 PACK_STEPS = 4
 
 
-def pack(fresh_qkv, peers, chosen):
+def pack(fresh_qkv, peers, runs):
     kinds, tokens, pairs, width = fresh_qkv.shape
     here = pairs // peers
     columns = pairs // PACK_STEPS
-    rows = kinds * tokens * len(chosen)
-    part = (rows * columns // here, width)
+    part = (kinds * tokens * columns, width)
+    shapes = [(kinds * tokens * len(run) * peers, width) for run in runs]
     return pl.pallas_call(
-        functools.partial(pack_kernel, here, chosen),
-        out_shape=jax.ShapeDtypeStruct((rows * peers, width), fresh_qkv.dtype),
+        functools.partial(pack_kernel, here, runs),
+        out_shape=[jax.ShapeDtypeStruct(shape, fresh_qkv.dtype) for shape in shapes],
         in_specs=[ANY],
-        out_specs=ANY,
+        out_specs=[ANY] * len(runs),
         scratch_shapes=[
             pltpu.VMEM((PACK_STEPS, kinds, tokens, columns, width), fresh_qkv.dtype),
-            pltpu.VMEM((kinds * tokens * columns, width), F32),
+            pltpu.VMEM(part, F32),
             pltpu.VMEM(part, F32),
             pltpu.VMEM((PACK_STEPS, *part), fresh_qkv.dtype),
             pltpu.SemaphoreType.DMA((PACK_STEPS,)),
-            pltpu.SemaphoreType.DMA((PACK_STEPS,)),
+            pltpu.SemaphoreType.DMA((PACK_STEPS, len(runs))),
         ],
         compiler_params=pltpu.CompilerParams(vmem_limit_bytes=60 * MIB),
         cost_estimate=cost(6),
@@ -148,39 +156,37 @@
 
     def fetch(pair):
         slot = pair % 2
-        rows = pl.ds(0, length)
-        pairs = [
-            (fresh_ref.at[pair, 0], keys.at[slot, rows, :]),
-            (fresh_ref.at[pair, 1], values.at[slot, rows, lanes]),
-        ]
-        for step in range(1, groups):
-            group = lax.rem(own + step, groups)
-            source = pl.ds(pl.multiple_of(group * length, length), length)
-            rows = pl.ds(step * length, length)
-            pairs += [
-                (stale_ref.at[0, first_pair + pair, source, :], keys.at[slot, rows, :]),
-                (stale_ref.at[1, first_pair + pair, source, :], values.at[slot, rows, lanes]),
+        chosen = first_pair + pair
+        sides = []
+        for kind, target in ((0, keys.at[slot]), (1, values.at[slot])):
+            side = [(fresh_ref.at[pair, kind], target.at[pl.ds(0, length), lanes])]
+            for step in range(1, groups):
+                group = lax.rem(own + step, groups)
+                source = pl.ds(pl.multiple_of(group * length, length), length)
+                rows = pl.ds(step * length, length)
+                side.append((stale_ref.at[kind, chosen, source, :], target.at[rows, lanes]))
+            copies = [
+                pltpu.make_async_copy(src, dst, sems.at[slot, kind * groups + i])
+                for i, (src, dst) in enumerate(side)
             ]
-        copies = [
-            pltpu.make_async_copy(src, dst, sems.at[slot, i]) for i, (src, dst) in enumerate(pairs)
-        ]
-        for copy in copies:
-            copy.start()
-        return copies
+            for copy in copies:
+                copy.start()
+            sides.append(copies)
+        return sides
 
     def lay_out(pair, source):
         for t in range(tokens):
             rows = pl.ds(pair * tokens + t, peers, stride=here * tokens)
             sent[rows, :] = source[pl.ds(t, peers, stride=tokens), :]
 
-    def attend_pair(pair):
+    def attend_pair(pair, key_copies, value_copies):
         slot = pair % 2
         valid = counts[(own_pair + pair) // HEADS]
         shown = lax.broadcasted_iota(jnp.int32, (text_len, width), 0) < valid
+        for copy in key_copies:
+            copy.wait()
         text_keys = keys[slot, text, :].astype(F32)
         keys[slot, text, :] = jnp.where(shown, text_keys, text_keys[0:1]).astype(keys.dtype)
-        text_values = values[slot, text, lanes].astype(F32)
-        values[slot, text, lanes] = jnp.where(shown, text_values, 0.0).astype(values.dtype)
         values[slot, text, ones] = jnp.where(shown, 1.0, 0.0).astype(values.dtype)
 
         def score(i, side):
@@ -206,6 +212,10 @@
             result[pl.ds(i * BLOCK, BLOCK), :] = summed[:, :width] / summed[:, width:]
 
         top = score(0, 0)
+        for copy in value_copies:
+            copy.wait()
+        text_values = values[slot, text, lanes].astype(F32)
+        values[slot, text, lanes] = jnp.where(shown, text_values, 0.0).astype(values.dtype)
         for i in range(1, blocks):
             new_top = score(i, i % 2)
             weigh(i - 1, (i - 1) % 2, top)
@@ -218,11 +228,10 @@
         earlier = pltpu.make_async_copy(done_ref, done, done_sem)
         earlier.start()
     for pair in range(count):
-        for copy in waiting:
-            copy.wait()
+        ready = waiting
         if pair + 1 < count:
             waiting = fetch(pair + 1)
-        attend_pair(pair)
+        attend_pair(pair, *ready)
         if last:
             lay_out(first_pair + pair, result)
         else:
@@ -247,7 +256,8 @@
         out_shape = jax.ShapeDtypeStruct((here * length, width), query.dtype)
     else:
         out_shape = jax.ShapeDtypeStruct(query.shape, F32)
-    done = counts
+    if done is None:
+        done = counts
     return pl.pallas_call(
         functools.partial(attend_kernel, text_len, tokens, first_pair, here),
         out_shape=out_shape,
@@ -263,7 +273,7 @@
             pltpu.SemaphoreType.DMA((2, 2 * groups)),
             pltpu.SemaphoreType.DMA,
         ],
-        compiler_params=pltpu.CompilerParams(vmem_limit_bytes=36 * MIB),
+        compiler_params=pltpu.CompilerParams(vmem_limit_bytes=(57 if last else 36) * MIB),
         cost_estimate=cost(16, 8 * count * length * total * width, count * length * total),
         name="attend",
     )(counts, query, fresh, stale, done)
@@ -300,8 +310,9 @@
     kinds, here = o_ref.shape[:2]
     length = o_ref.shape[2] // groups
     own = lax.axis_index("patch").astype(jnp.int32)
-    sources = [[ref.at[pair] for pair in range(here)] for ref in part_refs[: groups - 1]]
-    sources.append([ref.at[0] for ref in part_refs[groups - 1 :]])
+    sources = [[] for _ in range(groups)]
+    for i, ref in enumerate(part_refs):
+        sources[i % groups] += [ref.at[pair] for pair in range(ref.shape[0])]
     reads, writes = [], []
     for pair in range(here):
         for kind in range(kinds):
@@ -325,13 +336,13 @@
         copy.wait()
 
 
-def place(parts, far_near, here, groups):
+def place(parts, here, groups):
     _, kinds, length, width = parts[0].shape
     shape = (kinds, here, groups * length, width)
     return pl.pallas_call(
         functools.partial(place_kernel, groups),
         out_shape=jax.ShapeDtypeStruct(shape, parts[0].dtype),
-        in_specs=[ANY] * (len(parts) + here),
+        in_specs=[ANY] * len(parts),
         out_specs=ANY,
         scratch_shapes=[
             pltpu.VMEM(shape, parts[0].dtype),
@@ -341,7 +352,7 @@
         compiler_params=pltpu.CompilerParams(vmem_limit_bytes=16 * MIB),
         cost_estimate=cost(1),
         name="place",
-    )(*parts, *far_near)
+    )(*parts)
 
 
 def exchange(rows):
@@ -364,14 +375,22 @@
     text_len = TXT_DEV * seq_len // (TXT_DEV + IMG_DEV)
     stale = jnp.transpose(stale_kv, (0, 2, 1, 3))
 
-    every = tuple(range(here))
-    query, fresh = unpack(exchange(pack(fresh_qkv, peers, every)), here)
+    early, late = tuple(range(here - 1)), (here - 1,)
+    early_sent, late_sent = pack(fresh_qkv, peers, (early, late))
+    query, fresh = unpack(exchange(early_sent), len(early))
+    late_sent, query = lax.optimization_barrier((late_sent, query))
+    received = exchange(late_sent)
     far = swap(fresh, 2)
-    attended = attend(text_count, query, fresh, stale, None, 0, text_len, tokens)
+    done = attend(text_count, query, fresh, stale, None, 0, text_len, tokens)
+    received, done = lax.optimization_barrier((received, done))
+    query, late_fresh = unpack(received, len(late))
+    late_far = swap(late_fresh, 2)
+    attended = attend(text_count, query, late_fresh, stale, done, len(early), text_len, tokens)
     moved = exchange(attended)
-    far, _ = lax.optimization_barrier((far, attended))
-    far_near = [swap(far[pair : pair + 1], 1) for pair in range(here)]
-    refreshed = place([fresh, swap(fresh, 1), far], far_near, here, groups)
+    far, late_far, _ = lax.optimization_barrier((far, late_far, attended))
+    parts = [fresh, swap(fresh, 1), far, swap(far, 1)]
+    parts += [late_fresh, swap(late_fresh, 1), late_far, swap(late_far, 1)]
+    refreshed = place(parts, here, groups)
     moved, refreshed = lax.optimization_barrier((moved, refreshed))
     result = merge(moved, pairs)
     return (result, jnp.transpose(refreshed, (0, 2, 1, 3)))

time: 139 us -> 140 us (level)
  blocking collectives: 76.5 us -> 57.2 us
  starting transfers between devices: 8.01 us -> 17.2 us
  local copies, waits for them, and re-layouts: 0.12 us -> 6.61 us
  Pallas kernels: 31.6 us -> 34.8 us
    all_to_all x1, blocking collectives: 76.5 us -> 57.2 us  [exchange(): lax.all_to_all(two_rows, 'seq', split_axis=0, concat_axis=0, tiled=True)]
    all_to_all x1 -> x2, waiting for transfers between devices: 0.77 us -> 12.7 us  [exchange(): lax.all_to_all(two_rows, 'seq', split_axis=0, concat_axis=0, tiled=True)]
    ppermute x5 -> x6, waiting for transfers between devices: 20.3 us -> 9.85 us  [swap(): return lax.ppermute(array, 'patch', [(g, g ^ bit) for g in range(groups)])]
    all_to_all x1 -> x2, starting transfers between devices: 6.43 us -> 14.9 us  [exchange(): lax.all_to_all(two_rows, 'seq', split_axis=0, concat_axis=0, tiled=True)]
    unnamed x4 -> x12, local copies, waits for them, and re-layouts: 0.01 us -> 6.61 us
    pallas_call x1 -> x2, Pallas kernels: 21.3 us -> 24.1 us  [attend(): pl.pallas_call(functools.partial(attend_kernel, text_len, tokens, first_p...]
  transfers between devices with their start and end apart: 6 -> 8, of which waited for: 5 -> 5; matrix products, arithmetic and copies ran while one was open for 0% -> 0% of each run, Pallas kernels for 19% -> 21%
where the time goes in v4:
time: 140 us; the launch traced here: 139 us
  blocking collectives  57.2 us (41%)
  Pallas kernels  34.8 us (25%)
  waiting for transfers between devices  22.5 us (16%)
  starting transfers between devices  17.2 us (12%)
  local copies, waits for them, and re-layouts  6.61 us (5%)
    all_to_all x1, blocking collectives, exchange(): lax.all_to_all(two_rows, 'seq', split_axis=0, concat_axis=0, tiled=True)  57.2 us
    pallas_call x2, Pallas kernels, attend(): pl.pallas_call(functools.partial(attend_kernel, text_len, tokens, first_p...  24.1 us
    all_to_all x2, starting transfers between devices, exchange(): lax.all_to_all(two_rows, 'seq', split_axis=0, concat_axis=0, tiled=True)  14.9 us
    all_to_all x2, waiting for transfers between devices, exchange(): lax.all_to_all(two_rows, 'seq', split_axis=0, concat_axis=0, tiled=True)  12.7 us
    ppermute x6, waiting for transfers between devices, swap(): return lax.ppermute(array, 'patch', [(g, g ^ bit) for g in range(groups)])  9.85 us
    unnamed x12, local copies, waits for them, and re-layouts  6.61 us
    pallas_call x1, Pallas kernels, place(): pl.pallas_call(functools.partial(place_kernel, groups), out_shape=jax.Sha...  4.4 us
    pallas_call x1, Pallas kernels, pack(): pl.pallas_call(functools.partial(pack_kernel, here, runs), out_shape=[jax...  2.99 us
  transfers between devices with their start and end apart: 8, of which 5 were waited for; matrix products, arithmetic and copies ran while one was open for 0% of the time, Pallas kernels for 21%

profile of v4, /device:TPU:4, one launch (start us, length us, event | category | flops | bytes accessed | tf_op | source)
XLA Modules:
  0.0 139.1 jit_solution(11514080510397738524)
XLA Ops:
  0.6 3.0 %pack.1 = (bf16[6912,128]{1,0:T(8,128)(2,1)}, bf16[3456,128]{1,0:T(8,128)(2,1)}) custom-call(bf16[3,18,192,128]{3,2,1,0:T(8,128)(2,1)} %x_ref.1), custom_call_target="tpu_custom_call" | custom-call | bytes 6291456 | tf_op jit(solution)/shard_map/pack/pallas_call | solution.py:75
  3.6 57.2 %all_to_all.15 = bf16[3456,2,128]{2,1,0:T(2,128)(2,1)S(1)} all-to-all(bf16[3456,2,128]{2,1,0:T(2,128)(2,1)} %bitcast.14), channel_id=1, replica_groups=mesh['patch'=4,'seq'=64] {'seq'}, dimensions={0} | all-to-all | bytes 3538944 | tf_op jit(solution)/shard_map/all_to_all | solution.py:360
  60.8 0.0 copy-start.4
  60.8 1.0 unpack.2
  61.8 0.0 copy-start.1
  61.8 0.8 copy-done.1
  62.6 5.9 %all-to-all-start.1 = ((bf16[1728,2,128]{2,1,0:T(2,128)(2,1)}), bf16[1728,2,128]{2,1,0:T(2,128)(2,1)S(1)}, u32[]{:S(2)}, u32[]{:S(2)}) async-start(bf16[1728,2,128]{2,1,0:T(2,128)(2,1)} %bitcast.16), calls=%async_computation.1 | async-start | bytes 1769472 | tf_op jit(solution)/shard_map/all_to_all | solution.py:360
  68.5 0.9 collective-permute-start.1
  69.4 0.0 copy-done.4
  69.4 0.0 copy-start
  69.4 3.0 %copy-done = bf16[2,4608,3,128]{3,1,2,0:T(8,128)(2,1)S(1)} copy-done((bf16[2,4608,3,128]{3,1,2,0:T(8,128)(2,1)S(1)}, bf16[2,4608,3,128]{3,1,2,0:T(8,128)(2,1)}, u32[]{:S(2)}) %copy-start) | copy-done | bytes 7077912
  72.4 0.0 copy-start.2
  72.4 1.1 copy-done.2
  73.5 14.5 %attend.2.done_ref = f32[2,1152,128]{2,1,0:T(8,128)S(1)} custom-call(s32[8]{0:T(128)S(1)} %copy-done.4, bf16[2,1152,128]{2,1,0:T(8,128)(2,1)S(1)} %copy-done.2, bf16[2,2,1152,128]{3,2,1,0:T(8,128)(2,1)S(1)} %get-tuple-element.21.fresh_ref.refs_0_, bf16[2,3,4608,128]{3,2,1,0:T(8,128)(2,1)S(1)} %bitcast.12, s32[8]{0:T(128)S(1)} %copy-done.4), custom_call_target="tpu_custom_call" | custom-call | flops 10871635968 | bytes 16777216 | tf_op jit(solution)/shard_map/attend/pallas_call | solution.py:261
  88.0 0.0 copy-start.5
  88.0 1.0 copy-done.5
  89.0 4.2 %all-to-all-done.1 = bf16[1728,2,128]{2,1,0:T(2,128)(2,1)S(1)} async-done(((bf16[1728,2,128]{2,1,0:T(2,128)(2,1)}), bf16[1728,2,128]{2,1,0:T(2,128)(2,1)S(1)}, u32[]{:S(2)}, u32[]{:S(2)}) %all-to-all-start.1) | async-done | bytes 884768 | tf_op jit(solution)/shard_map/all_to_all | solution.py:360
  93.3 1.1 unpack.3
  94.4 0.0 copy-start.3
  94.4 0.7 copy-done.3
  95.1 0.8 collective-permute-start.2
  95.9 9.5 %attend.3 = bf16[3456,128]{1,0:T(8,128)(2,1)} custom-call(s32[8]{0:T(128)} %counts.3, bf16[1,1152,128]{2,1,0:T(8,128)(2,1)} %copy-done.3, bf16[1,2,1152,128]{3,2,1,0:T(8,128)(2,1)} %get-tuple-element.24.fresh_ref.refs_4_, bf16[2,3,4608,128]{3,2,1,0:T(8,128)(2,1)} %bitcast.11, f32[2,1152,128]{2,1,0:T(8,128)} %copy-done.5), custom_call_target="tpu_custom_call" | custom-call | flops 5435817984 | bytes 16777216 | tf_op jit(solution)/shard_map/attend/pallas_call | solution.py:261
  105.4 9.0 %all-to-all-start.2 = ((bf16[1728,2,128]{2,1,0:T(2,128)(2,1)}), bf16[1728,2,128]{2,1,0:T(2,128)(2,1)S(1)}, u32[]{:S(2)}, u32[]{:S(2)}) async-start(bf16[1728,2,128]{2,1,0:T(2,128)(2,1)} %bitcast.15), calls=%async_computation.2 | async-start | bytes 1769472 | tf_op jit(solution)/shard_map/all_to_all | solution.py:360
  114.5 0.1 collective-permute-start
  114.6 0.0 collective-permute-done.1.refs_2_
  114.6 5.6 %collective-permute-done.2.refs_6_ = bf16[1,2,1152,128]{3,2,1,0:T(8,128)(2,1)} collective-permute-done((bf16[1,2,1152,128]{3,2,1,0:T(8,128)(2,1)}, bf16[1,2,1152,128]{3,2,1,0:T(8,128)(2,1)}, u32[]{:S(2)}, u32[]{:S(2)}) %collective-permute-start.2) | collective-permute-done | bytes 589856 | tf_op jit(solution)/shard_map/ppermute | solution.py:366
  120.2 0.0 collective-permute-start.3
  120.2 0.5 collective-permute-start.4
  120.7 0.0 collective-permute-start.5
  120.7 0.0 collective-permute-done.refs_1_
  120.7 3.0 %collective-permute-done.4.refs_5_ = bf16[1,2,1152,128]{3,2,1,0:T(8,128)(2,1)S(1)} collective-permute-done((bf16[1,2,1152,128]{3,2,1,0:T(8,128)(2,1)}, bf16[1,2,1152,128]{3,2,1,0:T(8,128)(2,1)S(1)}, u32[]{:S(2)}, u32[]{:S(2)}) %collective-permute-start.4) | collective-permute-done | bytes 589856 | tf_op jit(solution)/shard_map/ppermute | solution.py:366
  123.7 1.2 collective-permute-done.5.refs_7_
  124.9 0.0 collective-permute-done.3.refs_3_
  124.9 4.4 %place.1 = bf16[2,3,4608,128]{3,2,1,0:T(8,128)(2,1)} custom-call(bf16[2,2,1152,128]{3,2,1,0:T(8,128)(2,1)S(1)} %get-tuple-element.21.fresh_ref.refs_0_, bf16[2,2,1152,128]{3,2,1,0:T(8,128)(2,1)S(1)} %collective-permute-done.refs_1_, bf16[2,2,1152,128]{3,2,1,0:T(8,128)(2,1)S(1)} %collective-permute-done.1.refs_2_, ...), custom_call_target="tpu_custom_call" | custom-call | bytes 1048576 | tf_op jit(solution)/shard_map/place/pallas_call | solution.py:342
  129.3 8.5 %all-to-all-done.2 = bf16[1728,2,128]{2,1,0:T(2,128)(2,1)S(1)} async-done(((bf16[1728,2,128]{2,1,0:T(2,128)(2,1)}), bf16[1728,2,128]{2,1,0:T(2,128)(2,1)S(1)}, u32[]{:S(2)}, u32[]{:S(2)}) %all-to-all-start.2) | async-done | bytes 884768 | tf_op jit(solution)/shard_map/all_to_all | solution.py:360
  137.8 1.3 merge.1
Async XLA Ops:
  60.8 8.6 %copy-start.4 = (s32[8]{0:T(128)S(1)}, s32[8]{0:T(128)}, u32[]{:S(2)}) copy-start(s32[8]{0:T(128)} %counts.3) | copy-start | bytes 100
  61.8 0.8 copy-start.1
  62.6 30.6 %all-to-all-start.1 = ((bf16[1728,2,128]{2,1,0:T(2,128)(2,1)}), bf16[1728,2,128]{2,1,0:T(2,128)(2,1)S(1)}, u32[]{:S(2)}, u32[]{:S(2)}) async-start(bf16[1728,2,128]{2,1,0:T(2,128)(2,1)} %bitcast.16), calls=%async_computation.1 | async-start | bytes 1769472 | tf_op jit(solution)/shard_map/all_to_all | solution.py:360
  68.5 46.0 %collective-permute-start.1 = (bf16[2,2,1152,128]{3,2,1,0:T(8,128)(2,1)S(1)}, bf16[2,2,1152,128]{3,2,1,0:T(8,128)(2,1)S(1)}, u32[]{:S(2)}, u32[]{:S(2)}) collective-permute-start(bf16[2,2,1152,128]{3,2,1,0:T(8,128)(2,1)S(1)} %get-tuple-element.21.fresh_ref.refs_0_), channel_id=1, source_target_pairs={{0,128},{64,192},{128,0},{192,64},{1,129},{65,193},{129,1},{193,65... | collective-permute-start | bytes 3538952 | tf_op jit(solution)/shard_map/ppermute | solution.py:366
  69.4 3.0 %copy-start = (bf16[2,4608,3,128]{3,1,2,0:T(8,128)(2,1)S(1)}, bf16[2,4608,3,128]{3,1,2,0:T(8,128)(2,1)}, u32[]{:S(2)}) copy-start(bf16[2,4608,3,128]{3,1,2,0:T(8,128)(2,1)} %param.4) | copy-start | bytes 21233668
  72.4 1.1 copy-start.2
  88.0 1.0 copy-start.5
  94.4 0.7 copy-start.3
  95.1 25.1 %collective-permute-start.2 = (bf16[1,2,1152,128]{3,2,1,0:T(8,128)(2,1)}, bf16[1,2,1152,128]{3,2,1,0:T(8,128)(2,1)}, u32[]{:S(2)}, u32[]{:S(2)}) collective-permute-start(bf16[1,2,1152,128]{3,2,1,0:T(8,128)(2,1)} %get-tuple-element.24.fresh_ref.refs_4_), channel_id=1, source_target_pairs={{0,128},{64,192},{128,0},{192,64},{1,129},{65,193},{129,1},{193,65... | collective-permute-start | bytes 1769480 | tf_op jit(solution)/shard_map/ppermute | solution.py:366
  105.4 32.3 %all-to-all-start.2 = ((bf16[1728,2,128]{2,1,0:T(2,128)(2,1)}), bf16[1728,2,128]{2,1,0:T(2,128)(2,1)S(1)}, u32[]{:S(2)}, u32[]{:S(2)}) async-start(bf16[1728,2,128]{2,1,0:T(2,128)(2,1)} %bitcast.15), calls=%async_computation.2 | async-start | bytes 1769472 | tf_op jit(solution)/shard_map/all_to_all | solution.py:360
  114.5 6.2 %collective-permute-start = (bf16[2,2,1152,128]{3,2,1,0:T(8,128)(2,1)S(1)}, bf16[2,2,1152,128]{3,2,1,0:T(8,128)(2,1)S(1)}, u32[]{:S(2)}, u32[]{:S(2)}) collective-permute-start(bf16[2,2,1152,128]{3,2,1,0:T(8,128)(2,1)S(1)} %get-tuple-element.21.fresh_ref.refs_0_), channel_id=1, source_target_pairs={{0,64},{64,0},{128,192},{192,128},{1,65},{65,1},{129,193},{193,129... | collective-permute-start | bytes 3538952 | tf_op jit(solution)/shard_map/ppermute | solution.py:366
  120.2 4.7 %collective-permute-start.3 = (bf16[2,2,1152,128]{3,2,1,0:T(8,128)(2,1)S(1)}, bf16[2,2,1152,128]{3,2,1,0:T(8,128)(2,1)S(1)}, u32[]{:S(2)}, u32[]{:S(2)}) collective-permute-start(bf16[2,2,1152,128]{3,2,1,0:T(8,128)(2,1)S(1)} %collective-permute-done.1.refs_2_), channel_id=1, source_target_pairs={{0,64},{64,0},{128,192},{192,128},{1,65},{65,1},{129,193},{193,129... | collective-permute-start | bytes 3538952 | tf_op jit(solution)/shard_map/ppermute | solution.py:366
  120.2 3.5 %collective-permute-start.4 = (bf16[1,2,1152,128]{3,2,1,0:T(8,128)(2,1)}, bf16[1,2,1152,128]{3,2,1,0:T(8,128)(2,1)S(1)}, u32[]{:S(2)}, u32[]{:S(2)}) collective-permute-start(bf16[1,2,1152,128]{3,2,1,0:T(8,128)(2,1)} %get-tuple-element.24.fresh_ref.refs_4_), channel_id=1, source_target_pairs={{0,64},{64,0},{128,192},{192,128},{1,65},{65,1},{129,193},{193,129... | collective-permute-start | bytes 1769480 | tf_op jit(solution)/shard_map/ppermute | solution.py:366
  120.7 4.2 %collective-permute-start.5 = (bf16[1,2,1152,128]{3,2,1,0:T(8,128)(2,1)}, bf16[1,2,1152,128]{3,2,1,0:T(8,128)(2,1)S(1)}, u32[]{:S(2)}, u32[]{:S(2)}) collective-permute-start(bf16[1,2,1152,128]{3,2,1,0:T(8,128)(2,1)} %collective-permute-done.2.refs_6_), channel_id=1, source_target_pairs={{0,64},{64,0},{128,192},{192,128},{1,65},{65,1},{129,193},{193,129... | collective-permute-start | bytes 1769480 | tf_op jit(solution)/shard_map/ppermute | solution.py:366

commit v5 on v4

--- a/solution.py
+++ b/solution.py
@@ -91,8 +91,8 @@
     )(fresh_qkv)
 
 
-def unpack_kernel(here, x_ref, q_ref, fresh_out, wide, ordered, both, sems):
-    length = q_ref.shape[1]
+def unpack_kernel(here, x_ref, q_out, fresh_out, wide, ordered, query, both, sems):
+    length = query.shape[1]
     tokens = TOKENS
     peers = length // tokens
     wide[...] = x_ref[...].astype(F32)
@@ -105,12 +105,13 @@
                     block = wide[pl.ds(row, peers, stride=here * KINDS * tokens), :]
                     ordered[c, pl.ds(t, peers, stride=tokens), :] = block
             if len(kinds) == 1:
-                q_ref[j] = ordered[0].astype(q_ref.dtype)
+                query[j] = ordered[0].astype(query.dtype)
+                copy = pltpu.make_async_copy(query.at[j], q_out.at[j], sems.at[here + j])
             else:
                 both[j] = ordered[1:].astype(both.dtype)
                 copy = pltpu.make_async_copy(both.at[j], fresh_out.at[j], sems.at[j])
-                copy.start()
-                copies.append(copy)
+            copy.start()
+            copies.append(copy)
     for copy in copies:
         copy.wait()
 
@@ -127,12 +128,13 @@
         functools.partial(unpack_kernel, here),
         out_shape=[jax.ShapeDtypeStruct(shape, dtype) for shape in shapes],
         in_specs=[VMEM],
-        out_specs=[VMEM, HBM],
+        out_specs=[HBM, HBM],
         scratch_shapes=[
             pltpu.VMEM((total, width), F32),
             pltpu.VMEM((KINDS, length, width), F32),
+            pltpu.VMEM((here, length, width), dtype),
             pltpu.VMEM((here, 2, length, width), dtype),
-            pltpu.SemaphoreType.DMA((here,)),
+            pltpu.SemaphoreType.DMA((2 * here,)),
         ],
         compiler_params=pltpu.CompilerParams(vmem_limit_bytes=16 * MIB),
         cost_estimate=cost(5),
@@ -141,7 +143,7 @@
 
 
 def attend_kernel(text_len, tokens, first_pair, here, counts, q_ref, fresh_ref, stale_ref, done_ref, o_ref,
-                  keys, values, scores, result, done, sent, sems, done_sem):
+                  query, keys, values, scores, result, done, sent, sems, done_sem):
     count, length, width = q_ref.shape
     total = keys.shape[1]
     groups = total // length
@@ -160,13 +162,15 @@
         sides = []
         for kind, target in ((0, keys.at[slot]), (1, values.at[slot])):
             side = [(fresh_ref.at[pair, kind], target.at[pl.ds(0, length), lanes])]
+            if kind == 0:
+                side.append((q_ref.at[pair], query.at[slot]))
             for step in range(1, groups):
                 group = lax.rem(own + step, groups)
                 source = pl.ds(pl.multiple_of(group * length, length), length)
                 rows = pl.ds(step * length, length)
                 side.append((stale_ref.at[kind, chosen, source, :], target.at[rows, lanes]))
             copies = [
-                pltpu.make_async_copy(src, dst, sems.at[slot, kind * groups + i])
+                pltpu.make_async_copy(src, dst, sems.at[slot, kind * (groups + 1) + i])
                 for i, (src, dst) in enumerate(side)
             ]
             for copy in copies:
@@ -190,7 +194,7 @@
         values[slot, text, ones] = jnp.where(shown, 1.0, 0.0).astype(values.dtype)
 
         def score(i, side):
-            rows = q_ref[pair, pl.ds(i * BLOCK, BLOCK), :]
+            rows = query[slot, pl.ds(i * BLOCK, BLOCK), :]
             dims = (((1,), (1,)), ((), ()))
             top = None
             for at in range(0, total, CHUNK):
@@ -216,11 +220,19 @@
             copy.wait()
         text_values = values[slot, text, lanes].astype(F32)
         values[slot, text, lanes] = jnp.where(shown, text_values, 0.0).astype(values.dtype)
+        if last and pair == 0:
+            lay_out_earlier()
         for i in range(1, blocks):
             new_top = score(i, i % 2)
             weigh(i - 1, (i - 1) % 2, top)
             top = new_top
         weigh(blocks - 1, (blocks - 1) % 2, top)
+
+    def lay_out_earlier():
+        if first_pair:
+            earlier.wait()
+        for pair in range(first_pair):
+            lay_out(pair, done.at[pair])
 
     waiting = fetch(0)
     values[:, :, ones] = jnp.ones((2, total, width), values.dtype)
@@ -237,10 +249,6 @@
         else:
             o_ref[pair] = result[...]
     if last:
-        if first_pair:
-            earlier.wait()
-        for pair in range(first_pair):
-            lay_out(pair, done.at[pair])
         o_ref[...] = sent[...].astype(o_ref.dtype)
 
 
@@ -261,16 +269,17 @@
     return pl.pallas_call(
         functools.partial(attend_kernel, text_len, tokens, first_pair, here),
         out_shape=out_shape,
-        in_specs=[pl.BlockSpec(memory_space=pltpu.SMEM), VMEM, HBM, HBM, ANY],
+        in_specs=[pl.BlockSpec(memory_space=pltpu.SMEM), HBM, HBM, HBM, ANY],
         out_specs=VMEM,
         scratch_shapes=[
+            pltpu.VMEM((2, length, width), query.dtype),
             pltpu.VMEM((2, total, width), query.dtype),
             pltpu.VMEM((2, total, 2 * width), query.dtype),
             pltpu.VMEM((2, BLOCK, total), F32),
             pltpu.VMEM((length, width), F32),
             pltpu.VMEM(done.shape, done.dtype),
             pltpu.VMEM((here * length, width), F32),
-            pltpu.SemaphoreType.DMA((2, 2 * groups)),
+            pltpu.SemaphoreType.DMA((2, 2 * groups + 1)),
             pltpu.SemaphoreType.DMA,
         ],
         compiler_params=pltpu.CompilerParams(vmem_limit_bytes=(57 if last else 36) * MIB),

time: 140 us -> 140 us (level)
  no operation moved by 1% of the time
where the time goes in v5:
time: 140 us; the launch traced here: 139 us
  blocking collectives  57.2 us (41%)
  Pallas kernels  34.8 us (25%)
  waiting for transfers between devices  22.4 us (16%)
  starting transfers between devices  17.3 us (12%)
  local copies, waits for them, and re-layouts  6.61 us (5%)
    all_to_all x1, blocking collectives, exchange(): lax.all_to_all(two_rows, 'seq', split_axis=0, concat_axis=0, tiled=True)  57.2 us
    pallas_call x2, Pallas kernels, attend(): pl.pallas_call(functools.partial(attend_kernel, text_len, tokens, first_p...  23.9 us
    all_to_all x2, starting transfers between devices, exchange(): lax.all_to_all(two_rows, 'seq', split_axis=0, concat_axis=0, tiled=True)  15 us
    all_to_all x2, waiting for transfers between devices, exchange(): lax.all_to_all(two_rows, 'seq', split_axis=0, concat_axis=0, tiled=True)  12.4 us
    ppermute x6, waiting for transfers between devices, swap(): return lax.ppermute(array, 'patch', [(g, g ^ bit) for g in range(groups)])  10 us
    unnamed x12, local copies, waits for them, and re-layouts  6.61 us
    pallas_call x1, Pallas kernels, place(): pl.pallas_call(functools.partial(place_kernel, groups), out_shape=jax.Sha...  4.4 us
    pallas_call x1, Pallas kernels, pack(): pl.pallas_call(functools.partial(pack_kernel, here, runs), out_shape=[jax...  2.99 us
  transfers between devices with their start and end apart: 8, of which 5 were waited for; matrix products, arithmetic and copies ran while one was open for 0% of the time, Pallas kernels for 21%

profile of v5, /device:TPU:4, one launch (start us, length us, event | category | flops | bytes accessed | tf_op | source)
XLA Modules:
  0.0 139.1 jit_solution(17364361953894890667)
XLA Ops:
  0.6 3.0 %pack.1 = (bf16[6912,128]{1,0:T(8,128)(2,1)}, bf16[3456,128]{1,0:T(8,128)(2,1)}) custom-call(bf16[3,18,192,128]{3,2,1,0:T(8,128)(2,1)} %x_ref.1), custom_call_target="tpu_custom_call" | custom-call | bytes 6291456 | tf_op jit(solution)/shard_map/pack/pallas_call | solution.py:75
  3.6 57.2 %all_to_all.15 = bf16[3456,2,128]{2,1,0:T(2,128)(2,1)S(1)} all-to-all(bf16[3456,2,128]{2,1,0:T(2,128)(2,1)} %bitcast.14), channel_id=1, replica_groups=mesh['patch'=4,'seq'=64] {'seq'}, dimensions={0} | all-to-all | bytes 3538944 | tf_op jit(solution)/shard_map/all_to_all | solution.py:369
  60.8 0.0 copy-start.4
  60.8 1.1 unpack.2
  62.0 0.0 copy-start.1
  62.0 0.8 copy-done.1
  62.8 5.9 %all-to-all-start.1 = ((bf16[1728,2,128]{2,1,0:T(2,128)(2,1)}), bf16[1728,2,128]{2,1,0:T(2,128)(2,1)S(1)}, u32[]{:S(2)}, u32[]{:S(2)}) async-start(bf16[1728,2,128]{2,1,0:T(2,128)(2,1)} %bitcast.16), calls=%async_computation.1 | async-start | bytes 1769472 | tf_op jit(solution)/shard_map/all_to_all | solution.py:369
  68.7 0.9 collective-permute-start.1
  69.5 0.0 copy-done.4
  69.5 0.0 copy-start
  69.6 3.0 %copy-done = bf16[2,4608,3,128]{3,1,2,0:T(8,128)(2,1)S(1)} copy-done((bf16[2,4608,3,128]{3,1,2,0:T(8,128)(2,1)S(1)}, bf16[2,4608,3,128]{3,1,2,0:T(8,128)(2,1)}, u32[]{:S(2)}) %copy-start) | copy-done | bytes 7077912
  72.6 0.0 copy-start.2
  72.6 1.1 copy-done.2
  73.6 14.7 %attend.2.done_ref = f32[2,1152,128]{2,1,0:T(8,128)S(1)} custom-call(s32[8]{0:T(128)S(1)} %copy-done.4, bf16[2,1152,128]{2,1,0:T(8,128)(2,1)S(1)} %copy-done.2, bf16[2,2,1152,128]{3,2,1,0:T(8,128)(2,1)S(1)} %get-tuple-element.21.fresh_ref.refs_0_, bf16[2,3,4608,128]{3,2,1,0:T(8,128)(2,1)S(1)} %bitcast.12, s32[8]{0:T(128)S(1)} %copy-done.4), custom_call_target="tpu_custom_call" | custom-call | flops 10871635968 | bytes 16777216 | tf_op jit(solution)/shard_map/attend/pallas_call | solution.py:269
  88.3 0.0 copy-start.5
  88.3 1.0 copy-done.5
  89.3 4.1 %all-to-all-done.1 = bf16[1728,2,128]{2,1,0:T(2,128)(2,1)S(1)} async-done(((bf16[1728,2,128]{2,1,0:T(2,128)(2,1)}), bf16[1728,2,128]{2,1,0:T(2,128)(2,1)S(1)}, u32[]{:S(2)}, u32[]{:S(2)}) %all-to-all-start.1) | async-done | bytes 884768 | tf_op jit(solution)/shard_map/all_to_all | solution.py:369
  93.4 1.1 unpack.3
  94.5 0.0 copy-start.3
  94.5 0.7 copy-done.3
  95.3 0.8 collective-permute-start.2
  96.1 9.3 %attend.3 = bf16[3456,128]{1,0:T(8,128)(2,1)} custom-call(s32[8]{0:T(128)} %counts.3, bf16[1,1152,128]{2,1,0:T(8,128)(2,1)} %copy-done.3, bf16[1,2,1152,128]{3,2,1,0:T(8,128)(2,1)} %get-tuple-element.24.fresh_ref.refs_4_, bf16[2,3,4608,128]{3,2,1,0:T(8,128)(2,1)} %bitcast.11, f32[2,1152,128]{2,1,0:T(8,128)} %copy-done.5), custom_call_target="tpu_custom_call" | custom-call | flops 5435817984 | bytes 16777216 | tf_op jit(solution)/shard_map/attend/pallas_call | solution.py:269
  105.3 9.2 %all-to-all-start.2 = ((bf16[1728,2,128]{2,1,0:T(2,128)(2,1)}), bf16[1728,2,128]{2,1,0:T(2,128)(2,1)S(1)}, u32[]{:S(2)}, u32[]{:S(2)}) async-start(bf16[1728,2,128]{2,1,0:T(2,128)(2,1)} %bitcast.15), calls=%async_computation.2 | async-start | bytes 1769472 | tf_op jit(solution)/shard_map/all_to_all | solution.py:369
  114.5 0.1 collective-permute-start
  114.6 0.0 collective-permute-done.1.refs_2_
  114.6 5.8 %collective-permute-done.2.refs_6_ = bf16[1,2,1152,128]{3,2,1,0:T(8,128)(2,1)} collective-permute-done((bf16[1,2,1152,128]{3,2,1,0:T(8,128)(2,1)}, bf16[1,2,1152,128]{3,2,1,0:T(8,128)(2,1)}, u32[]{:S(2)}, u32[]{:S(2)}) %collective-permute-start.2) | collective-permute-done | bytes 589856 | tf_op jit(solution)/shard_map/ppermute | solution.py:375
  120.4 0.0 collective-permute-start.3
  120.4 0.5 collective-permute-start.4
  120.9 0.0 collective-permute-start.5
  120.9 0.0 collective-permute-done.refs_1_
  120.9 3.0 %collective-permute-done.4.refs_5_ = bf16[1,2,1152,128]{3,2,1,0:T(8,128)(2,1)S(1)} collective-permute-done((bf16[1,2,1152,128]{3,2,1,0:T(8,128)(2,1)}, bf16[1,2,1152,128]{3,2,1,0:T(8,128)(2,1)S(1)}, u32[]{:S(2)}, u32[]{:S(2)}) %collective-permute-start.4) | collective-permute-done | bytes 589856 | tf_op jit(solution)/shard_map/ppermute | solution.py:375
  123.9 1.2 collective-permute-done.5.refs_7_
  125.1 0.0 collective-permute-done.3.refs_3_
  125.1 4.4 %place.1 = bf16[2,3,4608,128]{3,2,1,0:T(8,128)(2,1)} custom-call(bf16[2,2,1152,128]{3,2,1,0:T(8,128)(2,1)S(1)} %get-tuple-element.21.fresh_ref.refs_0_, bf16[2,2,1152,128]{3,2,1,0:T(8,128)(2,1)S(1)} %collective-permute-done.refs_1_, bf16[2,2,1152,128]{3,2,1,0:T(8,128)(2,1)S(1)} %collective-permute-done.1.refs_2_, ...), custom_call_target="tpu_custom_call" | custom-call | bytes 1048576 | tf_op jit(solution)/shard_map/place/pallas_call | solution.py:351
  129.6 8.3 %all-to-all-done.2 = bf16[1728,2,128]{2,1,0:T(2,128)(2,1)S(1)} async-done(((bf16[1728,2,128]{2,1,0:T(2,128)(2,1)}), bf16[1728,2,128]{2,1,0:T(2,128)(2,1)S(1)}, u32[]{:S(2)}, u32[]{:S(2)}) %all-to-all-start.2) | async-done | bytes 884768 | tf_op jit(solution)/shard_map/all_to_all | solution.py:369
  137.8 1.3 merge.1
Async XLA Ops:
  60.8 8.7 %copy-start.4 = (s32[8]{0:T(128)S(1)}, s32[8]{0:T(128)}, u32[]{:S(2)}) copy-start(s32[8]{0:T(128)} %counts.3) | copy-start | bytes 100
  62.0 0.8 copy-start.1
  62.8 30.6 %all-to-all-start.1 = ((bf16[1728,2,128]{2,1,0:T(2,128)(2,1)}), bf16[1728,2,128]{2,1,0:T(2,128)(2,1)S(1)}, u32[]{:S(2)}, u32[]{:S(2)}) async-start(bf16[1728,2,128]{2,1,0:T(2,128)(2,1)} %bitcast.16), calls=%async_computation.1 | async-start | bytes 1769472 | tf_op jit(solution)/shard_map/all_to_all | solution.py:369
  68.7 45.9 %collective-permute-start.1 = (bf16[2,2,1152,128]{3,2,1,0:T(8,128)(2,1)S(1)}, bf16[2,2,1152,128]{3,2,1,0:T(8,128)(2,1)S(1)}, u32[]{:S(2)}, u32[]{:S(2)}) collective-permute-start(bf16[2,2,1152,128]{3,2,1,0:T(8,128)(2,1)S(1)} %get-tuple-element.21.fresh_ref.refs_0_), channel_id=1, source_target_pairs={{0,128},{64,192},{128,0},{192,64},{1,129},{65,193},{129,1},{193,65... | collective-permute-start | bytes 3538952 | tf_op jit(solution)/shard_map/ppermute | solution.py:375
  69.5 3.0 %copy-start = (bf16[2,4608,3,128]{3,1,2,0:T(8,128)(2,1)S(1)}, bf16[2,4608,3,128]{3,1,2,0:T(8,128)(2,1)}, u32[]{:S(2)}) copy-start(bf16[2,4608,3,128]{3,1,2,0:T(8,128)(2,1)} %param.4) | copy-start | bytes 21233668
  72.6 1.1 copy-start.2
  88.3 1.0 copy-start.5
  94.5 0.7 copy-start.3
  95.3 25.1 %collective-permute-start.2 = (bf16[1,2,1152,128]{3,2,1,0:T(8,128)(2,1)}, bf16[1,2,1152,128]{3,2,1,0:T(8,128)(2,1)}, u32[]{:S(2)}, u32[]{:S(2)}) collective-permute-start(bf16[1,2,1152,128]{3,2,1,0:T(8,128)(2,1)} %get-tuple-element.24.fresh_ref.refs_4_), channel_id=1, source_target_pairs={{0,128},{64,192},{128,0},{192,64},{1,129},{65,193},{129,1},{193,65... | collective-permute-start | bytes 1769480 | tf_op jit(solution)/shard_map/ppermute | solution.py:375
  105.3 32.5 %all-to-all-start.2 = ((bf16[1728,2,128]{2,1,0:T(2,128)(2,1)}), bf16[1728,2,128]{2,1,0:T(2,128)(2,1)S(1)}, u32[]{:S(2)}, u32[]{:S(2)}) async-start(bf16[1728,2,128]{2,1,0:T(2,128)(2,1)} %bitcast.15), calls=%async_computation.2 | async-start | bytes 1769472 | tf_op jit(solution)/shard_map/all_to_all | solution.py:369
  114.5 6.4 %collective-permute-start = (bf16[2,2,1152,128]{3,2,1,0:T(8,128)(2,1)S(1)}, bf16[2,2,1152,128]{3,2,1,0:T(8,128)(2,1)S(1)}, u32[]{:S(2)}, u32[]{:S(2)}) collective-permute-start(bf16[2,2,1152,128]{3,2,1,0:T(8,128)(2,1)S(1)} %get-tuple-element.21.fresh_ref.refs_0_), channel_id=1, source_target_pairs={{0,64},{64,0},{128,192},{192,128},{1,65},{65,1},{129,193},{193,129... | collective-permute-start | bytes 3538952 | tf_op jit(solution)/shard_map/ppermute | solution.py:375
  120.4 4.7 %collective-permute-start.3 = (bf16[2,2,1152,128]{3,2,1,0:T(8,128)(2,1)S(1)}, bf16[2,2,1152,128]{3,2,1,0:T(8,128)(2,1)S(1)}, u32[]{:S(2)}, u32[]{:S(2)}) collective-permute-start(bf16[2,2,1152,128]{3,2,1,0:T(8,128)(2,1)S(1)} %collective-permute-done.1.refs_2_), channel_id=1, source_target_pairs={{0,64},{64,0},{128,192},{192,128},{1,65},{65,1},{129,193},{193,129... | collective-permute-start | bytes 3538952 | tf_op jit(solution)/shard_map/ppermute | solution.py:375
  120.4 3.5 %collective-permute-start.4 = (bf16[1,2,1152,128]{3,2,1,0:T(8,128)(2,1)}, bf16[1,2,1152,128]{3,2,1,0:T(8,128)(2,1)S(1)}, u32[]{:S(2)}, u32[]{:S(2)}) collective-permute-start(bf16[1,2,1152,128]{3,2,1,0:T(8,128)(2,1)} %get-tuple-element.24.fresh_ref.refs_4_), channel_id=1, source_target_pairs={{0,64},{64,0},{128,192},{192,128},{1,65},{65,1},{129,193},{193,129... | collective-permute-start | bytes 1769480 | tf_op jit(solution)/shard_map/ppermute | solution.py:375
  120.9 4.2 %collective-permute-start.5 = (bf16[1,2,1152,128]{3,2,1,0:T(8,128)(2,1)}, bf16[1,2,1152,128]{3,2,1,0:T(8,128)(2,1)S(1)}, u32[]{:S(2)}, u32[]{:S(2)}) collective-permute-start(bf16[1,2,1152,128]{3,2,1,0:T(8,128)(2,1)} %collective-permute-done.2.refs_6_), channel_id=1, source_target_pairs={{0,64},{64,0},{128,192},{192,128},{1,65},{65,1},{129,193},{193,129... | collective-permute-start | bytes 1769480 | tf_op jit(solution)/shard_map/ppermute | solution.py:375
